TPU v7x, 32 devices: a whole 2x2x4 slice. The times are simulated.
32 devices in a mesh: grp: 2 (over y), ri: 4 (over z), rj: 2 (over x), dp: 2 (over core).
Axes of the slice: x: 2, y: 2, z: 4, core: 2. Of those that a mesh axis runs over, the one named last changes fastest.
Arguments:
- homolog_activations: bfloat16 [64, 128, 256], P(('grp', 'ri', 'rj', 'dp')), parts along dimension 0, may hold values from -6 to 6
- homolog_tallies: int32 [256], P('grp'), parts along dimension 0, may hold values from 8 to 32, as said below
- standardize_gain: float32 [256], replicated, may hold values from 0.25 to 1.75
- standardize_offset: float32 [256], replicated, may hold values from -2.5 to 2.5
- former_factor_matrix: bfloat16 [256, 32], replicated, may hold values from -0.375 to 0.375
- former_factor_offset: float32 [32], replicated, may hold values from -2.5 to 2.5
- latter_factor_matrix: bfloat16 [256, 32], replicated, may hold values from -0.375 to 0.375
- latter_factor_offset: float32 [32], replicated, may hold values from -2.5 to 2.5
- pairwise_projection_matrix: float32 [1024, 128], replicated, may hold values from -3 to 3
Outputs:
- pair_update: float32 [256, 128, 128], P(('grp', 'ri'), ('rj', 'dp')), parts along dimension 0
There are 2 independent parts, one for each index of `grp`. A program takes and returns all parts, laid end to end along the dimension named above; an argument that names none is the same for every part. Nothing has to cross between parts.
Inputs may be any that keep to these rules, and one draw needn't show every extreme that they name: homolog_tallies[r] is the number of live MSA rows of residue r: rows 0 to homolog_tallies[r] - 1 are live, the others masked.
All inputs are finite; a program needn't handle non-finite values.
Results may differ from a plain program's by a relative error of at most 0.0049.
Values may be sent and summed in bfloat16 or wider, within the bound.
No kernel may reach another device: no remote copies, remote signals or barrier semaphores. Data moves between devices by JAX's collectives and lax.ppermute only.
A program may use at most 64 MiB of HBM per device.

v0:
```python
import math

import jax
import jax.numpy as jnp
from jax import lax
from jax.sharding import PartitionSpec as P


def pair_project(left_rows, right_rows, pairwise_projection_matrix, width):
    depth = left_rows.shape[0]
    first_count = left_rows.shape[1] // width
    second_count = right_rows.shape[1] // width
    lhs = left_rows.reshape(depth, first_count, width)
    rhs = right_rows.reshape(depth, second_count, width)
    block = math.gcd(first_count, max(1, 512 // second_count))

    def one_block(index):
        piece = lax.dynamic_slice_in_dim(lhs, index * block, block, 1)
        outer = jnp.einsum("sic,sje->ijce", piece, rhs, preferred_element_type=jnp.float32)
        projected = jnp.dot(
            outer.reshape(block * second_count, width * width),
            pairwise_projection_matrix,
            precision=lax.Precision.HIGHEST,
        )
        return projected.reshape(block, second_count, -1)

    blocks = lax.map(one_block, jnp.arange(first_count // block, dtype=jnp.int32))
    return blocks.reshape(first_count, second_count, -1)


def per_device(
    homolog_activations,
    homolog_tallies,
    standardize_gain,
    standardize_offset,
    former_factor_matrix,
    former_factor_offset,
    latter_factor_matrix,
    latter_factor_offset,
    pairwise_projection_matrix,
):
    width = former_factor_matrix.shape[1]
    occupied_homologs, chain_length, feature_width = homolog_activations.shape
    size_ri = lax.axis_size("ri")
    size_rj = lax.axis_size("rj")
    size_dp = lax.axis_size("dp")
    block_id = (lax.axis_index("ri") * size_rj + lax.axis_index("rj")) * size_dp + lax.axis_index(
        "dp"
    )
    row_indices = block_id * occupied_homologs + jnp.arange(occupied_homologs, dtype=jnp.int32)
    live = (row_indices[:, None] < homolog_tallies[None, :]).astype(jnp.float32)
    nonzero_elements = homolog_activations.astype(jnp.float32)
    center = nonzero_elements - jnp.mean(nonzero_elements, axis=-1, keepdims=True)
    spread = jnp.mean(center * center, axis=-1, keepdims=True)
    normalized_input = (
        center * lax.rsqrt(spread + 1e-05) * standardize_gain + standardize_offset
    ).astype(jnp.bfloat16)
    flattened = normalized_input.reshape(occupied_homologs * chain_length, feature_width)
    left_panel = jnp.dot(
        flattened, former_factor_matrix, preferred_element_type=jnp.float32
    ).reshape(occupied_homologs, chain_length, width)
    left_panel = (
        ((left_panel + former_factor_offset) * live[:, :, None])
        .astype(jnp.bfloat16)
        .reshape(occupied_homologs, chain_length * width)
    )
    right_panel = jnp.dot(
        flattened, latter_factor_matrix, preferred_element_type=jnp.float32
    ).reshape(occupied_homologs, chain_length, width)
    right_panel = (
        ((right_panel + latter_factor_offset) * live[:, :, None])
        .astype(jnp.bfloat16)
        .reshape(occupied_homologs, chain_length * width)
    )
    left_rows = lax.all_to_all(left_panel, "ri", split_axis=1, concat_axis=0, tiled=True)
    left_all = lax.all_gather(left_rows, "rj", axis=0, tiled=True)
    right_rows = lax.all_to_all(right_panel, "rj", split_axis=1, concat_axis=0, tiled=True)
    right_all = lax.all_gather(right_rows, "ri", axis=0, tiled=True)
    panel_cols = left_all.shape[1]
    left_all = left_all.reshape(size_rj, size_ri, occupied_homologs, panel_cols)
    left_all = jnp.transpose(left_all, (1, 0, 2, 3)).reshape(
        size_ri * size_rj * occupied_homologs, panel_cols
    )
    first_count = left_all.shape[1] // width
    second_count = right_all.shape[1] // width
    own_count = second_count // size_dp
    projected = pair_project(left_all, right_all, pairwise_projection_matrix, width)
    summed = lax.psum_scatter(projected, "dp", scatter_dimension=1, tiled=True)
    first_counts = lax.dynamic_slice_in_dim(
        homolog_tallies, lax.axis_index("ri") * first_count, first_count, 0
    )
    second_start = lax.axis_index("rj") * second_count + lax.axis_index("dp") * own_count
    second_counts = lax.dynamic_slice_in_dim(homolog_tallies, second_start, own_count, 0)
    bound = jnp.minimum(first_counts[:, None], second_counts[None, :]).astype(jnp.float32)
    return summed / (bound[:, :, None] + 0.001)


def solution(mesh):
    placed = (P(("grp", "ri", "rj", "dp"), None, None), P("grp"), P(), P(), P(), P(), P(), P(), P())
    return jax.shard_map(
        per_device,
        mesh=mesh,
        in_specs=placed,
        out_specs=P(("grp", "ri"), ("rj", "dp"), None),
        check_vma=False,
    )
```

profile of v0, /device:TPU:0, one launch (start us, length us, event | category | flops | bytes accessed | tf_op | source)
XLA Modules:
  0.0 108.4 jit_solution(13154617194014028830)
XLA Ops:
  6.5 1.0 convert_reduce_fusion
  7.6 1.1 %fusion.9 = f32[2,128]{1,0:T(2,128)S(1)} fusion(bf16[2,128,256]{2,1,0:T(8,128)(2,1)} %param.11, f32[2,128]{1,0:T(2,128)S(1)} %broadcast_multiply_fusion), kind=kLoop, calls=%fused_computation.17 | loop fusion | flops 261888 | bytes 133120 | tf_op jit(solution)/shard_map/reduce_sum | solution.py:54
  8.7 0.7 compare_convert_fusion
  9.4 1.2 %fusion.6 = bf16[2,128,32]{1,2,0:T(8,128)(2,1)S(1)} fusion(bf16[2,128,256]{2,1,0:T(8,128)(2,1)} %param.11, f32[256]{0:T(256)} %param.14, f32[256]{0:T(256)} %param.13, f32[2,128]{1,0:T(2,128)S(1)} %add_rsqrt_fusion, f32[2,128]{1,0:T(2,128)S(1)} %broadcast_multiply_fusion, bf16[256,32]{0,1:T(8,128)(2,1)S(1)} %copy-done, f32[32]{0:T(128)} %param.18, ...), kind=kOutput, calls=%fused_computation.12 | convolution fusion | flops 4612096 | bytes 169088 | tf_op jit(solution)/shard_map/dot_general | solution.py:67
  10.9 0.6 copy.25
  11.5 4.2 %all-to-all-start.1 = ((bf16[2,2,2048]{2,0,1:T(2,128)(2,1)}), bf16[2,2,2048]{2,0,1:T(2,128)(2,1)S(1)}, u32[]{:S(2)}, u32[]{:S(2)}) async-start(bf16[2,2,2048]{2,0,1:T(2,128)(2,1)} %copy.25), calls=%async_computation.1 | async-start | bytes 32768 | tf_op jit(solution)/shard_map/all_to_all | solution.py:77
  15.7 1.2 %fusion.5 = bf16[2,128,32]{1,2,0:T(8,128)(2,1)S(1)} fusion(bf16[2,128,256]{2,1,0:T(8,128)(2,1)} %param.11, f32[256]{0:T(256)} %param.14, f32[256]{0:T(256)} %param.13, f32[2,128]{1,0:T(2,128)S(1)} %add_rsqrt_fusion, f32[2,128]{1,0:T(2,128)S(1)} %broadcast_multiply_fusion, bf16[256,32]{0,1:T(8,128)(2,1)} %param.15, f32[2,128]{1,0:T(2,128)S(1)} %compare_convert_fusion, ...), kind=kOutput, calls=%fused_computation.11 | convolution fusion | flops 4612096 | bytes 169088 | tf_op jit(solution)/shard_map/dot_general | solution.py:59
  17.2 0.6 copy.22
  17.8 1.8 %all-to-all-done.1 = bf16[2,2,2048]{2,0,1:T(2,128)(2,1)S(1)} async-done(((bf16[2,2,2048]{2,0,1:T(2,128)(2,1)}), bf16[2,2,2048]{2,0,1:T(2,128)(2,1)S(1)}, u32[]{:S(2)}, u32[]{:S(2)}) %all-to-all-start.1) | async-done | bytes 16416 | tf_op jit(solution)/shard_map/all_to_all | solution.py:77
  19.6 5.3 %all-to-all-start = ((bf16[2,4,1024]{2,0,1:T(2,128)(2,1)}), bf16[2,4,1024]{2,0,1:T(2,128)(2,1)S(1)}, u32[]{:S(2)}, u32[]{:S(2)}) async-start(bf16[2,4,1024]{2,0,1:T(2,128)(2,1)} %copy.22), calls=%async_computation | async-start | bytes 32768 | tf_op jit(solution)/shard_map/all_to_all | solution.py:75
  24.9 13.7 %all-gather = bf16[4,4,2048]{2,1,0:T(4,128)(2,1)S(1)} all-gather(bf16[1,4,2048]{2,1,0:T(4,128)(2,1)S(1)} %reshape.118), channel_id=1, replica_groups=mesh['grp'=2,'ri'=4,'rj'=2,'dp'=2] {'ri'}, dimensions={0}, use_global_device_ids=true | all-gather | bytes 81920 | tf_op jit(solution)/shard_map/all_gather | solution.py:78
  38.6 0.2 reshape.116
  39.0 4.4 %all_gather.6 = bf16[16,1024]{1,0:T(8,128)(2,1)S(1)} all-gather(bf16[8,1024]{1,0:T(8,128)(2,1)S(1)} %all_to_all.31), channel_id=1, replica_groups=mesh['grp'=2,'ri'=4,'rj'=2,'dp'=2] {'rj'}, dimensions={0}, use_global_device_ids=true | all-gather | bytes 49152 | tf_op jit(solution)/shard_map/all_gather | solution.py:76
  43.6 47.1 %while.10 = (s32[]{:T(128)}, f32[4,8,64,128]{3,2,1,0:T(8,128)}, s32[4]{0:T(128)S(1)}, bf16[16,32,32]{2,1,0:T(8,128)(2,1)S(1)}, bf16[16,64,32]{1,0,2:T(8,128)(2,1...) while((s32[]{:T(128)}, f32[4,8,64,128]{3,2,1,0:T(8,128)}, ...), condition=%wide.region_3.4_spmd, body=%wide.region_2.3_spmd.sunk | while | flops 822083584 | bytes 11362507 | solution.py:27
  43.7 0.6 dynamic_slice.21
  44.9 0.7 convolution_bitcast_fusion.3
  45.7 2.4 %copy.38 = f32[8,64,32,32]{1,3,2,0:T(8,128)S(1)} copy(f32[8,64,32,32]{1,2,3,0:T(8,128)S(1)} %convolution_bitcast_fusion.3) | data formatting | bytes 4194304 | tf_op jit(solution)/shard_map/while/body/eval_jaxpr/sic,sje->ijce/transpose | solution.py:19
  48.1 7.4 %fusion.26 = f32[4,8,64,128]{3,2,1,0:T(8,128)} fusion(f32[4,8,64,128]{3,2,1,0:T(8,128)} %get-tuple-element.112, s32[]{:T(128)S(6)} %copy.42, f32[8,64,1024]{1,2,0:T(8,128)S(1)} %bitcast.48, f32[1024,128]{1,0:T(8,128)S(1)} %copy-done.1), kind=kOutput, calls=%fused_computation.2.clone.1 | convolution fusion | flops 805306368 | bytes 2883588 | tf_op jit(solution)/shard_map/while/body/eval_jaxpr/dot_general | solution.py:20
  55.4 0.6 dynamic_slice.21
  56.7 0.7 convolution_bitcast_fusion.3
  57.4 2.4 %copy.38 = f32[8,64,32,32]{1,3,2,0:T(8,128)S(1)} copy(f32[8,64,32,32]{1,2,3,0:T(8,128)S(1)} %convolution_bitcast_fusion.3) | data formatting | bytes 4194304 | tf_op jit(solution)/shard_map/while/body/eval_jaxpr/sic,sje->ijce/transpose | solution.py:19
  59.8 7.4 %fusion.26 = f32[4,8,64,128]{3,2,1,0:T(8,128)} fusion(f32[4,8,64,128]{3,2,1,0:T(8,128)} %get-tuple-element.112, s32[]{:T(128)S(6)} %copy.42, f32[8,64,1024]{1,2,0:T(8,128)S(1)} %bitcast.48, f32[1024,128]{1,0:T(8,128)S(1)} %copy-done.1), kind=kOutput, calls=%fused_computation.2.clone.1 | convolution fusion | flops 805306368 | bytes 2883588 | tf_op jit(solution)/shard_map/while/body/eval_jaxpr/dot_general | solution.py:20
  67.2 0.6 dynamic_slice.21
  68.5 0.7 convolution_bitcast_fusion.3
  69.2 2.4 %copy.38 = f32[8,64,32,32]{1,3,2,0:T(8,128)S(1)} copy(f32[8,64,32,32]{1,2,3,0:T(8,128)S(1)} %convolution_bitcast_fusion.3) | data formatting | bytes 4194304 | tf_op jit(solution)/shard_map/while/body/eval_jaxpr/sic,sje->ijce/transpose | solution.py:19
  71.6 7.4 %fusion.26 = f32[4,8,64,128]{3,2,1,0:T(8,128)} fusion(f32[4,8,64,128]{3,2,1,0:T(8,128)} %get-tuple-element.112, s32[]{:T(128)S(6)} %copy.42, f32[8,64,1024]{1,2,0:T(8,128)S(1)} %bitcast.48, f32[1024,128]{1,0:T(8,128)S(1)} %copy-done.1), kind=kOutput, calls=%fused_computation.2.clone.1 | convolution fusion | flops 805306368 | bytes 2883588 | tf_op jit(solution)/shard_map/while/body/eval_jaxpr/dot_general | solution.py:20
  79.0 0.6 dynamic_slice.21
  80.2 0.7 convolution_bitcast_fusion.3
  81.0 2.4 %copy.38 = f32[8,64,32,32]{1,3,2,0:T(8,128)S(1)} copy(f32[8,64,32,32]{1,2,3,0:T(8,128)S(1)} %convolution_bitcast_fusion.3) | data formatting | bytes 4194304 | tf_op jit(solution)/shard_map/while/body/eval_jaxpr/sic,sje->ijce/transpose | solution.py:19
  83.4 7.4 %fusion.26 = f32[4,8,64,128]{3,2,1,0:T(8,128)} fusion(f32[4,8,64,128]{3,2,1,0:T(8,128)} %get-tuple-element.112, s32[]{:T(128)S(6)} %copy.42, f32[8,64,1024]{1,2,0:T(8,128)S(1)} %bitcast.48, f32[1024,128]{1,0:T(8,128)S(1)} %copy-done.1), kind=kOutput, calls=%fused_computation.2.clone.1 | convolution fusion | flops 805306368 | bytes 2883588 | tf_op jit(solution)/shard_map/while/body/eval_jaxpr/dot_general | solution.py:20
  91.0 8.5 %reduce-scatter.2.cloned.1.call-done = f32[32,32,128]{2,1,0:T(8,128)} async-done(((f32[32,64,128]{2,1,0:T(8,128)}), f32[32,32,128]{2,1,0:T(8,128)}) %reduce-scatter.2.cloned.1.call-update) | async-done | bytes 524304 | tf_op jit(solution)/shard_map/reduce_scatter | solution.py:88
  99.5 2.0 %broadcast_divide_fusion = f32[32,32,128]{2,1,0:T(8,128)} fusion(f32[32,32,128]{2,1,0:T(8,128)} %reduce-scatter.2.cloned.1.call-done, f32[32,32]{1,0:T(8,128)S(1)} %convert_add_fusion), kind=kLoop, calls=%fused_computation.21 | loop fusion | flops 131072 | bytes 1052672 | tf_op jit(solution)/shard_map/div | solution.py:95
  (36 shorter events, 1.2 us)
Async XLA Ops:
  6.5 2.9 %copy-start = (bf16[256,32]{0,1:T(8,128)(2,1)S(1)}, bf16[256,32]{0,1:T(8,128)(2,1)}, u32[]{:S(2)}) copy-start(bf16[256,32]{0,1:T(8,128)(2,1)} %param.17) | copy-start | bytes 49156
  11.5 8.1 %all-to-all-start.1 = ((bf16[2,2,2048]{2,0,1:T(2,128)(2,1)}), bf16[2,2,2048]{2,0,1:T(2,128)(2,1)S(1)}, u32[]{:S(2)}, u32[]{:S(2)}) async-start(bf16[2,2,2048]{2,0,1:T(2,128)(2,1)} %copy.25), calls=%async_computation.1 | async-start | bytes 32768 | tf_op jit(solution)/shard_map/all_to_all | solution.py:77
  19.6 19.4 %all-to-all-start = ((bf16[2,4,1024]{2,0,1:T(2,128)(2,1)}), bf16[2,4,1024]{2,0,1:T(2,128)(2,1)S(1)}, u32[]{:S(2)}, u32[]{:S(2)}) async-start(bf16[2,4,1024]{2,0,1:T(2,128)(2,1)} %copy.22), calls=%async_computation | async-start | bytes 32768 | tf_op jit(solution)/shard_map/all_to_all | solution.py:75
  24.9 74.6 %reduce-scatter.2.cloned.1.call-start = ((), (), s32[]{:S(2)}) async-start(), calls=%async_computation.3 | async-start | bytes 1572864 | tf_op jit(solution)/shard_map/reduce_scatter | solution.py:88
  43.6 47.2 %copy-start.2 = (s32[128]{0:T(128)S(1)}, s32[128]{0:T(128)}, u32[]{:S(2)}) copy-start(s32[128]{0:T(128)} %param.12) | copy-start | bytes 1540
  45.6 2.4 %copy-start.1 = (f32[1024,128]{1,0:T(8,128)S(1)}, f32[1024,128]{1,0:T(8,128)}, u32[]{:S(2)}) copy-start(f32[1024,128]{1,0:T(8,128)} %get-tuple-element.126) | copy-start | bytes 1572868 | tf_op jit(solution)/shard_map/while
  57.4 2.4 %copy-start.1 = (f32[1024,128]{1,0:T(8,128)S(1)}, f32[1024,128]{1,0:T(8,128)}, u32[]{:S(2)}) copy-start(f32[1024,128]{1,0:T(8,128)} %get-tuple-element.126) | copy-start | bytes 1572868 | tf_op jit(solution)/shard_map/while
  69.2 2.4 %copy-start.1 = (f32[1024,128]{1,0:T(8,128)S(1)}, f32[1024,128]{1,0:T(8,128)}, u32[]{:S(2)}) copy-start(f32[1024,128]{1,0:T(8,128)} %get-tuple-element.126) | copy-start | bytes 1572868 | tf_op jit(solution)/shard_map/while
  81.0 2.4 %copy-start.1 = (f32[1024,128]{1,0:T(8,128)S(1)}, f32[1024,128]{1,0:T(8,128)}, u32[]{:S(2)}) copy-start(f32[1024,128]{1,0:T(8,128)} %get-tuple-element.126) | copy-start | bytes 1572868 | tf_op jit(solution)/shard_map/while
Sparse Core Ops, SparseCore 0:
  90.9 8.5 reduce-scatter.1
where the time goes:
time: 109 us; the launch traced here: 108 us
  matrix products  34.8 us (32%)
  blocking collectives  18.1 us (17%)
  local copies, waits for them, and re-layouts  14.3 us (13%)
  between operations  13.5 us (12%)
  waiting for transfers between devices  10.3 us (9%)
  starting transfers between devices  9.54 us (9%)
  other arithmetic  4.97 us (5%)
  loops' own time  2.77 us (3%)
    dot_general x4, matrix products, one_block(): jnp.dot(outer.reshape(block * second_count, width * width), pairwise_proj...  29.5 us
    all_gather x1, blocking collectives, per_device(): right_all = lax.all_gather(right_rows, 'ri', axis=0, tiled=True)  13.7 us
    transpose x4, local copies, waits for them, and re-layouts, one_block(): jnp.einsum('sic,sje->ijce', piece, rhs, preferred_element_type=jnp.float32)  9.5 us
    reduce_scatter x1, waiting for transfers between devices, per_device(): summed = lax.psum_scatter(projected, 'dp', scatter_dimension=1, tiled=True)  8.54 us
    all_to_all x1, starting transfers between devices, per_device(): lax.all_to_all(left_panel, 'ri', split_axis=1, concat_axis=0, tiled=True)  5.34 us
    all_gather x1, blocking collectives, per_device(): left_all = lax.all_gather(left_rows, 'rj', axis=0, tiled=True)  4.42 us
    all_to_all x1, starting transfers between devices, per_device(): lax.all_to_all(right_panel, 'rj', split_axis=1, concat_axis=0, tiled=True)  4.21 us
    dot_general x4, matrix products, one_block(): jnp.einsum('sic,sje->ijce', piece, rhs, preferred_element_type=jnp.float32)  2.91 us
  transfers between devices with their start and end apart: 3, of which 2 were waited for; matrix products, arithmetic and copies ran while one was open for 2% of the time, Pallas kernels for 0%

commit v1 on v0

v1 whole, which is shorter than its diff:
```python
import functools

import jax
import jax.numpy as jnp
from jax import lax
from jax.experimental import pallas as pl
from jax.experimental.pallas import tpu as pltpu
from jax.sharding import PartitionSpec as P

LANES = 128
TILE = 32
ROWS = 16


def span(masks):
    found = [0]
    for mask in masks:
        found += [f ^ mask for f in found]
    return found


def distinct(values):
    return sorted(set(values))


class Plan:
    def __init__(self, masks, split, left_unit, right_unit):
        self.masks = masks
        firsts = lambda ms: distinct(m // split for m in span(ms))
        seconds = lambda ms: distinct(m % split for m in span(ms))
        self.keep, self.send = [], []
        rest = masks[1:]
        left, right = {}, {}
        at = 0
        for p in firsts(rest):
            left[p] = [(0, at)]
            self.keep.append(("L", p))
            at += left_unit
        for p in seconds(rest):
            right[p] = [(0, at)]
            self.keep.append(("R", p))
            at += right_unit
        self.keep_rows = at
        v = masks[0]
        at = 0
        for p in firsts(rest):
            left[p].append((1, at))
            self.send.append(("L", p ^ (v // split)))
            at += left_unit
        for p in seconds(rest):
            right[p].append((1, at))
            self.send.append(("R", p ^ (v % split)))
            at += right_unit
        self.send_rows = at
        self.messages = []
        for step in range(1, len(masks)):
            v, rest = masks[step], masks[step + 1 :]
            message, at, number = [], 0, step + 1
            new_left, new_right = {}, {}
            for p in firsts(rest):
                new_left[p] = list(left[p])
                for buffer, row in left[p ^ (v // split)]:
                    message.append((buffer, row, left_unit))
                    new_left[p].append((number, at))
                    at += left_unit
            for p in seconds(rest):
                new_right[p] = list(right[p])
                for buffer, row in right[p ^ (v % split)]:
                    message.append((buffer, row, right_unit))
                    new_right[p].append((number, at))
                    at += right_unit
            merged = []
            for buffer, row, count in message:
                if merged and merged[-1][0] == buffer and merged[-1][1] + merged[-1][2] == row:
                    merged[-1] = (buffer, merged[-1][1], merged[-1][2] + count)
                else:
                    merged.append((buffer, row, count))
            self.messages.append(merged)
            left, right = new_left, new_right
        self.left, self.right = left[0], right[0]


def panels_kernel(
    plan, split, x_ref, tallies_ref, gain_ref, offset_ref, former_ref, former_bias_ref,
    latter_ref, latter_bias_ref, keep_ref, send_ref, left_ref, right_ref,
):
    depth, chain, features = x_ref.shape
    width = former_ref.shape[1]
    first = lax.axis_index("ri")
    second = lax.axis_index("rj") * lax.axis_size("dp") + lax.axis_index("dp")
    row_start = (first * split + second) * depth

    x = x_ref[...].reshape(depth * chain, features).astype(jnp.float32)
    center = x - jnp.mean(x, axis=-1, keepdims=True)
    spread = jnp.mean(center * center, axis=-1, keepdims=True)
    normed = center * lax.rsqrt(spread + 1e-05) * gain_ref[...] + offset_ref[...]
    normed = normed.astype(jnp.bfloat16)

    copies = LANES // width
    latter = latter_ref[...]
    former = former_ref[...]
    matrix = jnp.concatenate([latter] * copies + [former] * copies, axis=1)
    bias = jnp.concatenate([latter_bias_ref[...]] * copies + [former_bias_ref[...]] * copies, axis=1)
    both = jnp.dot(normed, matrix, preferred_element_type=jnp.float32) + bias

    tallies = tallies_ref[...]
    lane_block = lax.broadcasted_iota(jnp.int32, (8, LANES), 1) // TILE
    for chunk in range(chain // LANES):
        lanes = slice(chunk * LANES, (chunk + 1) * LANES)
        across = jnp.broadcast_to(tallies[:, lanes], (LANES, LANES)).astype(jnp.float32)
        down = across.T
        right_rows, left_rows = [], []
        for s in range(depth):
            row = (row_start + s).astype(jnp.float32)
            rows = slice(s * chain + chunk * LANES, s * chain + (chunk + 1) * LANES)
            right = both[rows, :LANES] * (row < down).astype(jnp.float32)
            left = both[rows, LANES:].T[:width] * (row < across[:width]).astype(jnp.float32)
            right_rows.append(right)
            left_rows.append(left)
        for b in range(LANES // TILE):
            tiles = []
            for s in range(depth):
                tile = None
                for q in range(copies):
                    part = right_rows[s][b * TILE + q * 8 : b * TILE + (q + 1) * 8]
                    tile = part if tile is None else jnp.where(lane_block == q, part, tile)
                tiles.append(tile)
            block = chunk * (LANES // TILE) + b
            right_ref[block * ROWS : (block + 1) * ROWS] = jnp.concatenate(tiles, 0).astype(jnp.bfloat16)
            tiles = []
            for s in range(depth):
                tile = None
                for q in range(copies):
                    part = left_rows[s][q * 8 : (q + 1) * 8]
                    shift = (q - b) * TILE % LANES
                    part = pltpu.roll(part, shift, 1) if shift else part
                    tile = part if tile is None else jnp.where(lane_block == q, part, tile)
                tiles.append(tile)
            left_ref[block * ROWS : (block + 1) * ROWS] = jnp.concatenate(tiles, 0).astype(jnp.bfloat16)

    right_unit = right_ref.shape[0] // split
    for out_ref, pieces in ((keep_ref, plan.keep), (send_ref, plan.send)):
        at = 0
        for kind, position in pieces:
            source, index, unit = (left_ref, first, ROWS) if kind == "L" else (right_ref, second, right_unit)
            start = pl.multiple_of((index ^ position) * unit, ROWS)
            out_ref[at : at + unit] = source[pl.ds(start, unit)]
            at += unit


def pairs_kernel(plan, first_count, second_count, *refs):
    buffers = refs[: len(plan.masks) + 1]
    matrix_ref, down_ref, tallies_ref, out_ref, gather_ref, left_ref, outer_ref, wide_ref = refs[len(plan.masks) + 1 :]
    first = lax.axis_index("ri")
    second = lax.axis_index("rj") * lax.axis_size("dp") + lax.axis_index("dp")
    step = pl.program_id(0)
    sources = len(plan.left)
    depth = sources * 2
    width = LANES // 4

    @pl.when(step == 0)
    def _():
        for k, (buffer, row) in enumerate(plan.left):
            gather_ref[k * ROWS : (k + 1) * ROWS] = buffers[buffer][row : row + ROWS].astype(jnp.float32)
        for half in range(2):
            stacked = jnp.concatenate(
                [gather_ref[pl.ds(half * 4 + c, depth, stride=8)] for c in range(4)], 0
            )
            left_ref[half * LANES : (half + 1) * LANES] = stacked.T.astype(jnp.bfloat16)
        matrix = matrix_ref[...]
        high = matrix.astype(jnp.bfloat16)
        wide_ref[:, :LANES] = high
        wide_ref[:, LANES:] = (matrix - high.astype(jnp.float32)).astype(jnp.bfloat16)

    for k, (buffer, row) in enumerate(plan.right):
        start = pl.multiple_of(row + step * ROWS, ROWS)
        gather_ref[k * ROWS : (k + 1) * ROWS] = buffers[buffer][pl.ds(start, ROWS)].astype(jnp.float32)
    left = left_ref[...]
    lane_block = lax.broadcasted_iota(jnp.int32, (depth, LANES), 1) // width
    for j8 in range(8):
        plain = gather_ref[pl.ds(j8, depth, stride=8)]
        turned = [plain] + [pltpu.roll(plain, r * width, 1) for r in range(1, 4)]
        for pair in range(2):
            columns = []
            for q in (2 * pair, 2 * pair + 1):
                columns.append(
                    jnp.concatenate(
                        [jnp.where(lane_block == c, turned[(c - q) % 4], 0.0) for c in range(4)], 0
                    )
                )
            spread = jnp.concatenate(columns, 1).astype(jnp.bfloat16)
            product = jnp.dot(left, spread, preferred_element_type=jnp.float32).astype(jnp.bfloat16)
            for at, q in enumerate((2 * pair, 2 * pair + 1)):
                j = q * 8 + j8
                for half in range(2):
                    for gq in range(4):
                        rows = (half * 4 + gq) * TILE
                        outer_ref[j * TILE : (j + 1) * TILE, (gq * 2 + half) * LANES : (gq * 2 + half + 1) * LANES] = (
                            product[rows : rows + TILE, at * LANES : (at + 1) * LANES]
                        )
    projected = jnp.dot(outer_ref[...], wide_ref[...], preferred_element_type=jnp.float32)
    projected = projected[:, :LANES] + projected[:, LANES:]
    first_tallies = jnp.broadcast_to(
        down_ref[pl.ds(pl.multiple_of(first * first_count, TILE), first_count)].astype(jnp.float32),
        (first_count, LANES),
    )
    for j in range(TILE):
        other = tallies_ref[second * second_count + step * TILE + j].astype(jnp.float32)
        bound = jnp.minimum(first_tallies, other) + 0.001
        out_ref[pl.ds(j, first_count, stride=TILE)] = projected[j * TILE : (j + 1) * TILE] / bound


def per_device(
    homolog_activations,
    homolog_tallies,
    standardize_gain,
    standardize_offset,
    former_factor_matrix,
    former_factor_offset,
    latter_factor_matrix,
    latter_factor_offset,
    pairwise_projection_matrix,
):
    depth, chain, features = homolog_activations.shape
    size_ri, size_rj, size_dp = (lax.axis_size(a) for a in ("ri", "rj", "dp"))
    split = size_rj * size_dp
    first_count, second_count = chain // size_ri, chain // split
    assert depth == 2 and first_count == TILE and second_count % TILE == 0 and chain % LANES == 0
    left_unit, right_unit = ROWS, ROWS * (second_count // TILE)
    total = size_ri * split
    masks = []
    bit = total // 2
    while bit:
        masks.append(bit if bit < size_dp else bit | (size_dp // 2))
        bit //= 2
    plan = Plan(masks, split, left_unit, right_unit)

    vmem = pl.BlockSpec(memory_space=pltpu.VMEM)
    bf16 = jnp.bfloat16
    keep, send = pl.pallas_call(
        functools.partial(panels_kernel, plan, split),
        out_shape=(
            jax.ShapeDtypeStruct((plan.keep_rows, LANES), bf16),
            jax.ShapeDtypeStruct((plan.send_rows, LANES), bf16),
        ),
        in_specs=[vmem] * 8,
        out_specs=(vmem, vmem),
        scratch_shapes=[
            pltpu.VMEM((chain // TILE * ROWS, LANES), bf16),
            pltpu.VMEM((chain // TILE * ROWS, LANES), bf16),
        ],
        compiler_params=pltpu.CompilerParams(vmem_limit_bytes=32 * 1024 * 1024),
        name="panels",
    )(
        homolog_activations,
        homolog_tallies[None, :],
        standardize_gain[None, :],
        standardize_offset[None, :],
        former_factor_matrix,
        former_factor_offset[None, :],
        latter_factor_matrix,
        latter_factor_offset[None, :],
    )

    axes = ("ri", "rj", "dp")
    swap = lambda v, m: lax.ppermute(v, axes, [(d, d ^ m) for d in range(total)])
    buffers = [keep, swap(send, masks[0])]
    for mask, pieces in zip(masks[1:], plan.messages):
        message = jnp.concatenate([buffers[b][r : r + n] for b, r, n in pieces], 0)
        buffers.append(swap(message, mask))

    blocks = second_count // TILE
    whole = lambda a: pl.BlockSpec(a.shape, lambda j: (0,) * a.ndim)
    down = homolog_tallies[:, None]
    out = pl.pallas_call(
        functools.partial(pairs_kernel, plan, first_count, second_count),
        grid=(blocks,),
        out_shape=jax.ShapeDtypeStruct((blocks, first_count * TILE, LANES), jnp.float32),
        in_specs=[whole(b) for b in buffers]
        + [whole(pairwise_projection_matrix), whole(down), pl.BlockSpec(memory_space=pltpu.SMEM)],
        out_specs=pl.BlockSpec((None, first_count * TILE, LANES), lambda j: (j, 0, 0)),
        scratch_shapes=[
            pltpu.VMEM((total * ROWS, LANES), jnp.float32),
            pltpu.VMEM((2 * LANES, 4 * total * 2), bf16),
            pltpu.VMEM((first_count * TILE, 8 * LANES), bf16),
            pltpu.VMEM((8 * LANES, 2 * LANES), bf16),
        ],
        compiler_params=pltpu.CompilerParams(vmem_limit_bytes=48 * 1024 * 1024),
        name="pairs",
    )(*buffers, pairwise_projection_matrix, down, homolog_tallies)
    out = out.reshape(blocks, first_count, TILE, LANES)
    if blocks == 1:
        return out[0]
    return jnp.transpose(out, (1, 0, 2, 3)).reshape(first_count, second_count, LANES)


def solution(mesh):
    placed = (P(("grp", "ri", "rj", "dp"), None, None), P("grp"), P(), P(), P(), P(), P(), P(), P())
    return jax.shard_map(
        per_device,
        mesh=mesh,
        in_specs=placed,
        out_specs=P(("grp", "ri"), ("rj", "dp"), None),
        check_vma=False,
    )
```

time: 109 us -> 23.6 us (0.22)
  the two profiles are of different devices: /device:TPU:0 before, /device:TPU:27 now
where the time goes in v1:
time: 23.6 us; the launch traced here: 23.2 us
  waiting for transfers between devices  11.8 us (50%)
  local copies, waits for them, and re-layouts  5.53 us (23%)
  Pallas kernels  3.9 us (17%)
  starting transfers between devices  1.86 us (8%)
    ppermute x4, waiting for transfers between devices, per_device(): lax.ppermute(v, axes, [(d, d ^ m) for d in range(total)])  11.8 us
    unnamed x39, local copies, waits for them, and re-layouts  5.41 us
    pallas_call x1, Pallas kernels, per_device(): pl.pallas_call(functools.partial(pairs_kernel, plan, first_count, second_...  3.2 us
    ppermute x4, starting transfers between devices, per_device(): lax.ppermute(v, axes, [(d, d ^ m) for d in range(total)])  1.86 us
    pallas_call x1, Pallas kernels, per_device(): pl.pallas_call(functools.partial(panels_kernel, plan, split), out_shape=(...  0.7 us
  transfers between devices with their start and end apart: 4, of which 4 were waited for; matrix products, arithmetic and copies ran while one was open for 0% of the time, Pallas kernels for 0%

profile of v1, /device:TPU:27, one launch (start us, length us, event | category | flops | bytes accessed | tf_op | source)
XLA Modules:
  0.0 23.2 jit_solution(10651658874365565114)
XLA Ops:
  0.0 0.0 copy-start.1
  0.0 0.0 copy-start
  0.0 0.9 %copy.10.former_ref = bf16[256,32]{1,0:T(8,128)(2,1)S(1)} copy(bf16[256,32]{0,1:T(8,128)(2,1)} %param.13) | data formatting | bytes 32768 | tf_op args[4]
  0.9 0.8 %copy.11.latter_ref = bf16[256,32]{1,0:T(8,128)(2,1)S(1)} copy(bf16[256,32]{0,1:T(8,128)(2,1)} %param.15) | data formatting | bytes 32768 | tf_op args[6]
  1.7 0.0 copy-done.1
  1.8 0.0 copy-start.2
  1.8 0.6 %copy-done.2 = s32[128]{0:T(128)S(1)} copy-done((s32[128]{0:T(128)S(1)}, s32[128]{0:T(128)}, u32[]{:S(2)}) %copy-start.2) | copy-done | bytes 536
  2.4 0.0 copy-start.4
  2.4 0.7 %copy-done.4 = f32[256]{0:T(256)S(1)} copy-done((f32[256]{0:T(256)S(1)}, f32[256]{0:T(256)}, u32[]{:S(2)}) %copy-start.4) | copy-done | bytes 1048
  3.1 0.0 copy-start.5
  3.1 0.7 %copy-done.5 = f32[256]{0:T(256)S(1)} copy-done((f32[256]{0:T(256)S(1)}, f32[256]{0:T(256)}, u32[]{:S(2)}) %copy-start.5) | copy-done | bytes 1048
  3.8 0.0 copy-start.6
  3.8 0.7 %copy-done.6 = f32[32]{0:T(128)S(1)} copy-done((f32[32]{0:T(128)S(1)}, f32[32]{0:T(128)}, u32[]{:S(2)}) %copy-start.6) | copy-done | bytes 152
  4.4 0.0 copy-start.7
  4.4 0.7 %copy-done.7 = f32[32]{0:T(128)S(1)} copy-done((f32[32]{0:T(128)S(1)}, f32[32]{0:T(128)}, u32[]{:S(2)}) %copy-start.7) | copy-done | bytes 152
  5.1 0.7 %panels.1 = (bf16[96,128]{1,0:T(8,128)(2,1)S(1)}, bf16[96,128]{1,0:T(8,128)(2,1)S(1)}) custom-call(bf16[2,128,256]{2,1,0:T(8,128)(2,1)S(1)} %copy-done.1, s32[1,128]{1,0:T(1,128)S(1)} %bitcast.7, f32[1,256]{1,0:T(1,128)S(1)} %bitcast.9, f32[1,256]{1,0:T(1,128)S(1)} %bitcast.10, bf16[256,32]{1,0:T(8,128)(2,1)S(1)} %copy.10.former_ref, f32[1,32]{1,0:T(1,128)S(1)} %bitcast.11, ...), custom_call_target="tpu_custom_call" | custom-call | tf_op jit(solution)/shard_map/panels/pallas_call | solution.py:240
  5.8 0.7 %collective-permute-start = (bf16[96,128]{1,0:T(8,128)(2,1)S(1)}, bf16[96,128]{1,0:T(8,128)(2,1)S(1)}, u32[]{:S(2)}, u32[]{:S(2)}) collective-permute-start(bf16[96,128]{1,0:T(8,128)(2,1)S(1)} %get-tuple-element.8), channel_id=1, source_target_pairs={{0,9},{1,8},{2,11},{3,10},{4,13},{5,12},{6,15},{7,14},{8,1},{9,0},... | collective-permute-start | bytes 73736 | tf_op jit(solution)/shard_map/ppermute | solution.py:266
  6.5 4.5 %collective-permute-done.refs_1_ = bf16[96,128]{1,0:T(8,128)(2,1)S(1)} collective-permute-done((bf16[96,128]{1,0:T(8,128)(2,1)S(1)}, bf16[96,128]{1,0:T(8,128)(2,1)S(1)}, u32[]{:S(2)}, u32[]{:S(2)}) %collective-permute-start) | collective-permute-done | bytes 24608 | tf_op jit(solution)/shard_map/ppermute | solution.py:266
  11.0 0.1 collective-permute-start.1
  11.2 3.5 %collective-permute-done.1.refs_2_ = bf16[160,128]{1,0:T(8,128)(2,1)S(1)} collective-permute-done((bf16[160,128]{1,0:T(8,128)(2,1)S(1)}, bf16[160,128]{1,0:T(8,128)(2,1)S(1)}, u32[]{:S(2)}, u32[]{:S(2)}) %collective-permute-start.1) | collective-permute-done | bytes 40992 | tf_op jit(solution)/shard_map/ppermute | solution.py:266
  14.7 0.6 %collective-permute-start.2 = (bf16[192,128]{1,0:T(8,128)(2,1)S(1)}, bf16[192,128]{1,0:T(8,128)(2,1)S(1)}, u32[]{:S(2)}, u32[]{:S(2)}) collective-permute-start(bf16[192,128]{1,0:T(8,128)(2,1)S(1)} %get-tuple-element.10), channel_id=1, source_target_pairs={{0,3},{1,2},{2,1},{3,0},{4,7},{5,6},{6,5},{7,4},{8,11},{9,10},{10,... | collective-permute-start | bytes 147464 | tf_op jit(solution)/shard_map/ppermute | solution.py:266
  15.3 3.2 %collective-permute-done.2.refs_3_ = bf16[192,128]{1,0:T(8,128)(2,1)S(1)} collective-permute-done((bf16[192,128]{1,0:T(8,128)(2,1)S(1)}, bf16[192,128]{1,0:T(8,128)(2,1)S(1)}, u32[]{:S(2)}, u32[]{:S(2)}) %collective-permute-start.2) | collective-permute-done | bytes 49184 | tf_op jit(solution)/shard_map/ppermute | solution.py:266
  18.6 0.0 copy-start.3
  18.6 0.5 %collective-permute-start.3 = (bf16[256,128]{1,0:T(8,128)(2,1)S(1)}, bf16[256,128]{1,0:T(8,128)(2,1)S(1)}, u32[]{:S(2)}, u32[]{:S(2)}) collective-permute-start(bf16[256,128]{1,0:T(8,128)(2,1)S(1)} %constant_dynamic-update-slice_fusion.19), channel_id=1, source_target_pairs={{0,1},{1,0},{2,3},{3,2},{4,5},{5,4},{6,7},{7,6},{8,9},{9,8},{10,11... | collective-permute-start | bytes 196616 | tf_op jit(solution)/shard_map/ppermute | solution.py:266
  19.1 0.2 copy-done.3
  19.3 0.1 copy.12.refs_6_
  19.4 0.6 %collective-permute-done.3.refs_4_ = bf16[256,128]{1,0:T(8,128)(2,1)S(1)} collective-permute-done((bf16[256,128]{1,0:T(8,128)(2,1)S(1)}, bf16[256,128]{1,0:T(8,128)(2,1)S(1)}, u32[]{:S(2)}, u32[]{:S(2)}) %collective-permute-start.3) | collective-permute-done | bytes 65568 | tf_op jit(solution)/shard_map/ppermute | solution.py:266
  20.0 0.0 copy-done
  20.0 3.2 %pairs.1 = f32[1,1024,128]{2,1,0:T(8,128)} custom-call(bf16[96,128]{1,0:T(8,128)(2,1)S(1)} %get-tuple-element.7.refs_0_, bf16[96,128]{1,0:T(8,128)(2,1)S(1)} %collective-permute-done.refs_1_, bf16[160,128]{1,0:T(8,128)(2,1)S(1)} %collective-permute-done.1.refs_2_, bf16[192,128]{1,0:T(8,128)(2,1)S(1)} %collective-permute-done.2.refs_3_, ...), custom_call_target="tpu_custom_call" | custom-call | tf_op jit(solution)/shard_map/pairs/pallas_call | solution.py:275
  (22 shorter events, 0.2 us)
Async XLA Ops:
  0.0 1.7 %copy-start.1 = (bf16[2,128,256]{2,1,0:T(8,128)(2,1)S(1)}, bf16[2,128,256]{2,1,0:T(8,128)(2,1)}, u32[]{:S(2)}) copy-start(bf16[2,128,256]{2,1,0:T(8,128)(2,1)} %x_ref.1) | copy-start | bytes 393220
  0.0 20.0 %copy-start = (f32[1024,128]{1,0:T(8,128)S(1)}, f32[1024,128]{1,0:T(8,128)}, u32[]{:S(2)}) copy-start(f32[1024,128]{1,0:T(8,128)} %refs_5_.1) | copy-start | bytes 1572868
  1.8 0.7 %copy-start.2 = (s32[128]{0:T(128)S(1)}, s32[128]{0:T(128)}, u32[]{:S(2)}) copy-start(s32[128]{0:T(128)} %refs_7_.1) | copy-start | bytes 1540
  2.4 0.7 %copy-start.4 = (f32[256]{0:T(256)S(1)}, f32[256]{0:T(256)}, u32[]{:S(2)}) copy-start(f32[256]{0:T(256)} %param.11) | copy-start | bytes 3076
  3.1 0.7 %copy-start.5 = (f32[256]{0:T(256)S(1)}, f32[256]{0:T(256)}, u32[]{:S(2)}) copy-start(f32[256]{0:T(256)} %param.12) | copy-start | bytes 3076
  3.8 0.7 %copy-start.6 = (f32[32]{0:T(128)S(1)}, f32[32]{0:T(128)}, u32[]{:S(2)}) copy-start(f32[32]{0:T(128)} %param.14) | copy-start | bytes 388
  4.4 0.7 %copy-start.7 = (f32[32]{0:T(128)S(1)}, f32[32]{0:T(128)}, u32[]{:S(2)}) copy-start(f32[32]{0:T(128)} %param.16) | copy-start | bytes 388
  5.8 5.2 %collective-permute-start = (bf16[96,128]{1,0:T(8,128)(2,1)S(1)}, bf16[96,128]{1,0:T(8,128)(2,1)S(1)}, u32[]{:S(2)}, u32[]{:S(2)}) collective-permute-start(bf16[96,128]{1,0:T(8,128)(2,1)S(1)} %get-tuple-element.8), channel_id=1, source_target_pairs={{0,9},{1,8},{2,11},{3,10},{4,13},{5,12},{6,15},{7,14},{8,1},{9,0},... | collective-permute-start | bytes 73736 | tf_op jit(solution)/shard_map/ppermute | solution.py:266
  11.0 3.6 %collective-permute-start.1 = (bf16[160,128]{1,0:T(8,128)(2,1)S(1)}, bf16[160,128]{1,0:T(8,128)(2,1)S(1)}, u32[]{:S(2)}, u32[]{:S(2)}) collective-permute-start(bf16[160,128]{1,0:T(8,128)(2,1)S(1)} %get-tuple-element.16), channel_id=1, source_target_pairs={{0,5},{1,4},{2,7},{3,6},{4,1},{5,0},{6,3},{7,2},{8,13},{9,12},{10,... | collective-permute-start | bytes 122888 | tf_op jit(solution)/shard_map/ppermute | solution.py:266
  14.7 3.8 %collective-permute-start.2 = (bf16[192,128]{1,0:T(8,128)(2,1)S(1)}, bf16[192,128]{1,0:T(8,128)(2,1)S(1)}, u32[]{:S(2)}, u32[]{:S(2)}) collective-permute-start(bf16[192,128]{1,0:T(8,128)(2,1)S(1)} %get-tuple-element.10), channel_id=1, source_target_pairs={{0,3},{1,2},{2,1},{3,0},{4,7},{5,6},{6,5},{7,4},{8,11},{9,10},{10,... | collective-permute-start | bytes 147464 | tf_op jit(solution)/shard_map/ppermute | solution.py:266
  18.6 0.7 %copy-start.3 = (s32[128]{0:T(128)S(1)}, s32[128]{0:T(128)}, u32[]{:S(2)}) copy-start(s32[128]{0:T(128)} %refs_7_.1) | copy-start | bytes 1540
  18.6 1.4 %collective-permute-start.3 = (bf16[256,128]{1,0:T(8,128)(2,1)S(1)}, bf16[256,128]{1,0:T(8,128)(2,1)S(1)}, u32[]{:S(2)}, u32[]{:S(2)}) collective-permute-start(bf16[256,128]{1,0:T(8,128)(2,1)S(1)} %constant_dynamic-update-slice_fusion.19), channel_id=1, source_target_pairs={{0,1},{1,0},{2,3},{3,2},{4,5},{5,4},{6,7},{7,6},{8,9},{9,8},{10,11... | collective-permute-start | bytes 196616 | tf_op jit(solution)/shard_map/ppermute | solution.py:266

commit v2 on v1

--- a/solution.py
+++ b/solution.py
@@ -10,6 +10,7 @@
 LANES = 128
 TILE = 32
 ROWS = 16
+VMEM_BYTES = 32 * 1024 * 1024
 
 
 def span(masks):
@@ -81,14 +82,26 @@
 
 
 def panels_kernel(
-    plan, split, x_ref, tallies_ref, gain_ref, offset_ref, former_ref, former_bias_ref,
-    latter_ref, latter_bias_ref, keep_ref, send_ref, left_ref, right_ref,
+    plan, split, x_hbm, tallies_hbm, gain_hbm, offset_hbm, former_hbm, former_bias_hbm, latter_hbm, latter_bias_hbm,
+    matrix_hbm, keep_ref, send_ref, first_ref, second_ref, matrix_ref,
+    x_ref, tallies_ref, gain_ref, offset_ref, former_ref, former_bias_ref, latter_ref, latter_bias_ref,
+    left_ref, right_ref, down_ref, sems,
 ):
     depth, chain, features = x_ref.shape
-    width = former_ref.shape[1]
+    width = former_ref.shape[0]
     first = lax.axis_index("ri")
     second = lax.axis_index("rj") * lax.axis_size("dp") + lax.axis_index("dp")
     row_start = (first * split + second) * depth
+
+    sources = (x_hbm, latter_hbm, former_hbm, gain_hbm, offset_hbm, tallies_hbm, latter_bias_hbm, former_bias_hbm)
+    targets = (x_ref, latter_ref, former_ref, gain_ref, offset_ref, tallies_ref, latter_bias_ref, former_bias_ref)
+    copies_in = [pltpu.make_async_copy(a, b, sems.at[k]) for k, (a, b) in enumerate(zip(sources, targets))]
+    matrix_copy = pltpu.make_async_copy(matrix_hbm, matrix_ref, sems.at[len(copies_in)])
+    for copy in copies_in:
+        copy.start()
+    matrix_copy.start()
+    for copy in copies_in:
+        copy.wait()
 
     x = x_ref[...].reshape(depth * chain, features).astype(jnp.float32)
     center = x - jnp.mean(x, axis=-1, keepdims=True)
@@ -99,9 +112,9 @@
     copies = LANES // width
     latter = latter_ref[...]
     former = former_ref[...]
-    matrix = jnp.concatenate([latter] * copies + [former] * copies, axis=1)
+    matrix = jnp.concatenate([latter] * copies + [former] * copies, axis=0)
     bias = jnp.concatenate([latter_bias_ref[...]] * copies + [former_bias_ref[...]] * copies, axis=1)
-    both = jnp.dot(normed, matrix, preferred_element_type=jnp.float32) + bias
+    both = lax.dot_general(normed, matrix, (((1,), (1,)), ((), ())), preferred_element_type=jnp.float32) + bias
 
     tallies = tallies_ref[...]
     lane_block = lax.broadcasted_iota(jnp.int32, (8, LANES), 1) // TILE
@@ -109,6 +122,7 @@
         lanes = slice(chunk * LANES, (chunk + 1) * LANES)
         across = jnp.broadcast_to(tallies[:, lanes], (LANES, LANES)).astype(jnp.float32)
         down = across.T
+        down_ref[lanes] = down
         right_rows, left_rows = [], []
         for s in range(depth):
             row = (row_start + s).astype(jnp.float32)
@@ -146,68 +160,69 @@
             start = pl.multiple_of((index ^ position) * unit, ROWS)
             out_ref[at : at + unit] = source[pl.ds(start, unit)]
             at += unit
+    for out_ref, index in ((first_ref, first), (second_ref, second)):
+        count = out_ref.shape[0]
+        out_ref[...] = down_ref[pl.ds(pl.multiple_of(index * count, TILE), count)]
+    matrix_copy.wait()
 
 
 def pairs_kernel(plan, first_count, second_count, *refs):
     buffers = refs[: len(plan.masks) + 1]
-    matrix_ref, down_ref, tallies_ref, out_ref, gather_ref, left_ref, outer_ref, wide_ref = refs[len(plan.masks) + 1 :]
-    first = lax.axis_index("ri")
-    second = lax.axis_index("rj") * lax.axis_size("dp") + lax.axis_index("dp")
-    step = pl.program_id(0)
+    matrix_ref, first_ref, second_ref, out_ref, gather_ref, left_ref, outer_ref, wide_ref = refs[len(plan.masks) + 1 :]
     sources = len(plan.left)
     depth = sources * 2
     width = LANES // 4
 
-    @pl.when(step == 0)
-    def _():
-        for k, (buffer, row) in enumerate(plan.left):
-            gather_ref[k * ROWS : (k + 1) * ROWS] = buffers[buffer][row : row + ROWS].astype(jnp.float32)
-        for half in range(2):
-            stacked = jnp.concatenate(
-                [gather_ref[pl.ds(half * 4 + c, depth, stride=8)] for c in range(4)], 0
-            )
-            left_ref[half * LANES : (half + 1) * LANES] = stacked.T.astype(jnp.bfloat16)
-        matrix = matrix_ref[...]
-        high = matrix.astype(jnp.bfloat16)
-        wide_ref[:, :LANES] = high
-        wide_ref[:, LANES:] = (matrix - high.astype(jnp.float32)).astype(jnp.bfloat16)
-
-    for k, (buffer, row) in enumerate(plan.right):
-        start = pl.multiple_of(row + step * ROWS, ROWS)
-        gather_ref[k * ROWS : (k + 1) * ROWS] = buffers[buffer][pl.ds(start, ROWS)].astype(jnp.float32)
-    left = left_ref[...]
-    lane_block = lax.broadcasted_iota(jnp.int32, (depth, LANES), 1) // width
-    for j8 in range(8):
-        plain = gather_ref[pl.ds(j8, depth, stride=8)]
-        turned = [plain] + [pltpu.roll(plain, r * width, 1) for r in range(1, 4)]
-        for pair in range(2):
-            columns = []
-            for q in (2 * pair, 2 * pair + 1):
-                columns.append(
-                    jnp.concatenate(
-                        [jnp.where(lane_block == c, turned[(c - q) % 4], 0.0) for c in range(4)], 0
+    for k, (buffer, row) in enumerate(plan.left):
+        gather_ref[k * ROWS : (k + 1) * ROWS] = buffers[buffer][row : row + ROWS].astype(jnp.float32)
+    for half in range(2):
+        stacked = jnp.concatenate([gather_ref[pl.ds(half * 4 + c, depth, stride=8)] for c in range(4)], 0)
+        left_ref[half * LANES : (half + 1) * LANES] = stacked.T.astype(jnp.bfloat16)
+    matrix = matrix_ref[...]
+    high = matrix.astype(jnp.bfloat16)
+    wide_ref[:, :LANES] = high
+    wide_ref[:, LANES:] = (matrix - high.astype(jnp.float32)).astype(jnp.bfloat16)
+    first_tallies = first_ref[...]
+
+    def one_block(block, carry):
+        for k, (buffer, row) in enumerate(plan.right):
+            start = pl.multiple_of(row + block * ROWS, ROWS)
+            gather_ref[k * ROWS : (k + 1) * ROWS] = buffers[buffer][pl.ds(start, ROWS)].astype(jnp.float32)
+        left = left_ref[...]
+        lane_block = lax.broadcasted_iota(jnp.int32, (depth, LANES), 1) // width
+        for j8 in range(8):
+            plain = gather_ref[pl.ds(j8, depth, stride=8)]
+            turned = [plain] + [pltpu.roll(plain, r * width, 1) for r in range(1, 4)]
+            for pair in range(2):
+                columns = []
+                for q in (2 * pair, 2 * pair + 1):
+                    columns.append(
+                        jnp.concatenate([jnp.where(lane_block == c, turned[(c - q) % 4], 0.0) for c in range(4)], 0)
                     )
-                )
-            spread = jnp.concatenate(columns, 1).astype(jnp.bfloat16)
-            product = jnp.dot(left, spread, preferred_element_type=jnp.float32).astype(jnp.bfloat16)
-            for at, q in enumerate((2 * pair, 2 * pair + 1)):
-                j = q * 8 + j8
-                for half in range(2):
-                    for gq in range(4):
-                        rows = (half * 4 + gq) * TILE
-                        outer_ref[j * TILE : (j + 1) * TILE, (gq * 2 + half) * LANES : (gq * 2 + half + 1) * LANES] = (
-                            product[rows : rows + TILE, at * LANES : (at + 1) * LANES]
-                        )
-    projected = jnp.dot(outer_ref[...], wide_ref[...], preferred_element_type=jnp.float32)
-    projected = projected[:, :LANES] + projected[:, LANES:]
-    first_tallies = jnp.broadcast_to(
-        down_ref[pl.ds(pl.multiple_of(first * first_count, TILE), first_count)].astype(jnp.float32),
-        (first_count, LANES),
-    )
-    for j in range(TILE):
-        other = tallies_ref[second * second_count + step * TILE + j].astype(jnp.float32)
-        bound = jnp.minimum(first_tallies, other) + 0.001
-        out_ref[pl.ds(j, first_count, stride=TILE)] = projected[j * TILE : (j + 1) * TILE] / bound
+                spread = jnp.concatenate(columns, 1).astype(jnp.bfloat16)
+                product = jnp.dot(left, spread, preferred_element_type=jnp.float32).astype(jnp.bfloat16)
+                for at, q in enumerate((2 * pair, 2 * pair + 1)):
+                    j = q * 8 + j8
+                    for half in range(2):
+                        for gq in range(4):
+                            rows = (half * 4 + gq) * TILE
+                            group = gq * 2 + half
+                            outer_ref[j * TILE : (j + 1) * TILE, group * LANES : (group + 1) * LANES] = (
+                                product[rows : rows + TILE, at * LANES : (at + 1) * LANES]
+                            )
+        projected = jnp.dot(outer_ref[...], wide_ref[...], preferred_element_type=jnp.float32)
+        projected = projected[:, :LANES] + projected[:, LANES:]
+        for j in range(TILE):
+            at = block * TILE + j
+            bound = jnp.minimum(first_tallies, second_ref[pl.ds(at, 1)]) + 0.001
+            out_ref[pl.ds(at, first_count, stride=second_count)] = projected[j * TILE : (j + 1) * TILE] / bound
+        return carry
+
+    blocks = second_count // TILE
+    if blocks == 1:
+        one_block(0, 0)
+    else:
+        lax.fori_loop(0, blocks, one_block, 0)
 
 
 def per_device(
@@ -236,31 +251,39 @@
     plan = Plan(masks, split, left_unit, right_unit)
 
     vmem = pl.BlockSpec(memory_space=pltpu.VMEM)
-    bf16 = jnp.bfloat16
-    keep, send = pl.pallas_call(
+    bf16, f32 = jnp.bfloat16, jnp.float32
+    operands = (
+        homolog_activations,
+        homolog_tallies[None, :],
+        standardize_gain[None, :],
+        standardize_offset[None, :],
+        former_factor_matrix.T,
+        former_factor_offset[None, :],
+        latter_factor_matrix.T,
+        latter_factor_offset[None, :],
+    )
+    in_hbm = [pltpu.with_memory_space_constraint(a, pltpu.HBM) for a in operands + (pairwise_projection_matrix,)]
+    keep, send, first_tallies, second_tallies, matrix = pl.pallas_call(
         functools.partial(panels_kernel, plan, split),
         out_shape=(
             jax.ShapeDtypeStruct((plan.keep_rows, LANES), bf16),
             jax.ShapeDtypeStruct((plan.send_rows, LANES), bf16),
+            jax.ShapeDtypeStruct((first_count, LANES), f32),
+            jax.ShapeDtypeStruct((second_count, LANES), f32),
+            jax.ShapeDtypeStruct(pairwise_projection_matrix.shape, f32),
         ),
-        in_specs=[vmem] * 8,
-        out_specs=(vmem, vmem),
-        scratch_shapes=[
+        in_specs=[pl.BlockSpec(memory_space=pltpu.HBM)] * len(in_hbm),
+        out_specs=(vmem,) * 5,
+        scratch_shapes=[pltpu.VMEM(a.shape, a.dtype) for a in operands]
+        + [
             pltpu.VMEM((chain // TILE * ROWS, LANES), bf16),
             pltpu.VMEM((chain // TILE * ROWS, LANES), bf16),
+            pltpu.VMEM((chain, LANES), f32),
+            pltpu.SemaphoreType.DMA((len(in_hbm),)),
         ],
-        compiler_params=pltpu.CompilerParams(vmem_limit_bytes=32 * 1024 * 1024),
+        compiler_params=pltpu.CompilerParams(vmem_limit_bytes=VMEM_BYTES),
         name="panels",
-    )(
-        homolog_activations,
-        homolog_tallies[None, :],
-        standardize_gain[None, :],
-        standardize_offset[None, :],
-        former_factor_matrix,
-        former_factor_offset[None, :],
-        latter_factor_matrix,
-        latter_factor_offset[None, :],
-    )
+    )(*in_hbm)
 
     axes = ("ri", "rj", "dp")
     swap = lambda v, m: lax.ppermute(v, axes, [(d, d ^ m) for d in range(total)])
@@ -269,29 +292,21 @@
         message = jnp.concatenate([buffers[b][r : r + n] for b, r, n in pieces], 0)
         buffers.append(swap(message, mask))
 
-    blocks = second_count // TILE
-    whole = lambda a: pl.BlockSpec(a.shape, lambda j: (0,) * a.ndim)
-    down = homolog_tallies[:, None]
     out = pl.pallas_call(
         functools.partial(pairs_kernel, plan, first_count, second_count),
-        grid=(blocks,),
-        out_shape=jax.ShapeDtypeStruct((blocks, first_count * TILE, LANES), jnp.float32),
-        in_specs=[whole(b) for b in buffers]
-        + [whole(pairwise_projection_matrix), whole(down), pl.BlockSpec(memory_space=pltpu.SMEM)],
-        out_specs=pl.BlockSpec((None, first_count * TILE, LANES), lambda j: (j, 0, 0)),
+        out_shape=jax.ShapeDtypeStruct((first_count * second_count, LANES), f32),
+        in_specs=[vmem] * (len(buffers) + 3),
+        out_specs=vmem,
         scratch_shapes=[
-            pltpu.VMEM((total * ROWS, LANES), jnp.float32),
+            pltpu.VMEM((total * ROWS, LANES), f32),
             pltpu.VMEM((2 * LANES, 4 * total * 2), bf16),
             pltpu.VMEM((first_count * TILE, 8 * LANES), bf16),
             pltpu.VMEM((8 * LANES, 2 * LANES), bf16),
         ],
-        compiler_params=pltpu.CompilerParams(vmem_limit_bytes=48 * 1024 * 1024),
+        compiler_params=pltpu.CompilerParams(vmem_limit_bytes=VMEM_BYTES),
         name="pairs",
-    )(*buffers, pairwise_projection_matrix, down, homolog_tallies)
-    out = out.reshape(blocks, first_count, TILE, LANES)
-    if blocks == 1:
-        return out[0]
-    return jnp.transpose(out, (1, 0, 2, 3)).reshape(first_count, second_count, LANES)
+    )(*buffers, matrix, first_tallies, second_tallies)
+    return out.reshape(first_count, second_count, LANES)
 
 
 def solution(mesh):

time: 23.6 us -> 18.5 us (0.78)
  the two profiles are of different devices: /device:TPU:27 before, /device:TPU:0 now
where the time goes in v2:
time: 18.5 us; the launch traced here: 18.1 us
  starting transfers between devices  7.74 us (42%)
  waiting for transfers between devices  6.03 us (33%)
  Pallas kernels  4.14 us (22%)
    ppermute x4, starting transfers between devices, per_device(): lax.ppermute(v, axes, [(d, d ^ m) for d in range(total)])  7.74 us
    ppermute x4, waiting for transfers between devices, per_device(): lax.ppermute(v, axes, [(d, d ^ m) for d in range(total)])  6.03 us
    pallas_call x1, Pallas kernels, per_device(): pl.pallas_call(functools.partial(pairs_kernel, plan, first_count, second_...  2.66 us
    pallas_call x1, Pallas kernels, per_device(): pl.pallas_call(functools.partial(panels_kernel, plan, split), out_shape=(...  1.47 us
  transfers between devices with their start and end apart: 4, of which 4 were waited for; matrix products, arithmetic and copies ran while one was open for 0% of the time, Pallas kernels for 0%

profile of v2, /device:TPU:0, one launch (start us, length us, event | category | flops | bytes accessed | tf_op | source)
XLA Modules:
  0.0 18.1 jit_solution(11774287480779272751)
XLA Ops:
  0.0 1.5 %panels.1 = (bf16[96,128]{1,0:T(8,128)(2,1)S(1)}, bf16[96,128]{1,0:T(8,128)(2,1)S(1)}, f32[32,128]{1,0:T(8,128)S(1)}, f32[32,128]{1,0:T(8,128)S(1)}, f32[1024,128]{1,0:T(8,128)S(1)}) custom-call(bf16[2,128,256]{2,1,0:T(8,128)(2,1)} %x_hbm.1, s32[1,128]{1,0:T(1,128)} %bitcast.12, f32[1,256]{1,0:T(1,128)} %bitcast.10, f32[1,256]{1,0:T(1,128)} %bitcast.11, ...), custom_call_target="tpu_custom_call" | custom-call | tf_op jit(solution)/shard_map/panels/pallas_call | solution.py:266
  1.5 3.5 %collective-permute-start = (bf16[96,128]{1,0:T(8,128)(2,1)S(1)}, bf16[96,128]{1,0:T(8,128)(2,1)S(1)}, u32[]{:S(2)}, u32[]{:S(2)}) collective-permute-start(bf16[96,128]{1,0:T(8,128)(2,1)S(1)} %get-tuple-element.11), channel_id=1, source_target_pairs={{0,9},{1,8},{2,11},{3,10},{4,13},{5,12},{6,15},{7,14},{8,1},{9,0},... | collective-permute-start | bytes 73736 | tf_op jit(solution)/shard_map/ppermute | solution.py:289
  5.0 1.6 %collective-permute-done.refs_1_ = bf16[96,128]{1,0:T(8,128)(2,1)S(1)} collective-permute-done((bf16[96,128]{1,0:T(8,128)(2,1)S(1)}, bf16[96,128]{1,0:T(8,128)(2,1)S(1)}, u32[]{:S(2)}, u32[]{:S(2)}) %collective-permute-start) | collective-permute-done | bytes 24608 | tf_op jit(solution)/shard_map/ppermute | solution.py:289
  6.7 1.9 %collective-permute-start.1 = (bf16[160,128]{1,0:T(8,128)(2,1)S(1)}, bf16[160,128]{1,0:T(8,128)(2,1)S(1)}, u32[]{:S(2)}, u32[]{:S(2)}) collective-permute-start(bf16[160,128]{1,0:T(8,128)(2,1)S(1)} %get-tuple-element.22), channel_id=1, source_target_pairs={{0,5},{1,4},{2,7},{3,6},{4,1},{5,0},{6,3},{7,2},{8,13},{9,12},{10,... | collective-permute-start | bytes 122888 | tf_op jit(solution)/shard_map/ppermute | solution.py:289
  8.6 1.7 %collective-permute-done.1.refs_2_ = bf16[160,128]{1,0:T(8,128)(2,1)S(1)} collective-permute-done((bf16[160,128]{1,0:T(8,128)(2,1)S(1)}, bf16[160,128]{1,0:T(8,128)(2,1)S(1)}, u32[]{:S(2)}, u32[]{:S(2)}) %collective-permute-start.1) | collective-permute-done | bytes 40992 | tf_op jit(solution)/shard_map/ppermute | solution.py:289
  10.4 1.9 %collective-permute-start.2 = (bf16[192,128]{1,0:T(8,128)(2,1)S(1)}, bf16[192,128]{1,0:T(8,128)(2,1)S(1)}, u32[]{:S(2)}, u32[]{:S(2)}) collective-permute-start(bf16[192,128]{1,0:T(8,128)(2,1)S(1)} %get-tuple-element.16), channel_id=1, source_target_pairs={{0,3},{1,2},{2,1},{3,0},{4,7},{5,6},{6,5},{7,4},{8,11},{9,10},{10,... | collective-permute-start | bytes 147464 | tf_op jit(solution)/shard_map/ppermute | solution.py:289
  12.2 1.8 %collective-permute-done.2.refs_3_ = bf16[192,128]{1,0:T(8,128)(2,1)S(1)} collective-permute-done((bf16[192,128]{1,0:T(8,128)(2,1)S(1)}, bf16[192,128]{1,0:T(8,128)(2,1)S(1)}, u32[]{:S(2)}, u32[]{:S(2)}) %collective-permute-start.2) | collective-permute-done | bytes 49184 | tf_op jit(solution)/shard_map/ppermute | solution.py:289
  14.1 0.4 %collective-permute-start.3 = (bf16[256,128]{1,0:T(8,128)(2,1)S(1)}, bf16[256,128]{1,0:T(8,128)(2,1)S(1)}, u32[]{:S(2)}, u32[]{:S(2)}) collective-permute-start(bf16[256,128]{1,0:T(8,128)(2,1)S(1)} %constant_dynamic-update-slice_fusion.19), channel_id=1, source_target_pairs={{0,1},{1,0},{2,3},{3,2},{4,5},{5,4},{6,7},{7,6},{8,9},{9,8},{10,11... | collective-permute-start | bytes 196616 | tf_op jit(solution)/shard_map/ppermute | solution.py:289
  14.5 0.9 %collective-permute-done.3.refs_4_ = bf16[256,128]{1,0:T(8,128)(2,1)S(1)} collective-permute-done((bf16[256,128]{1,0:T(8,128)(2,1)S(1)}, bf16[256,128]{1,0:T(8,128)(2,1)S(1)}, u32[]{:S(2)}, u32[]{:S(2)}) %collective-permute-start.3) | collective-permute-done | bytes 65568 | tf_op jit(solution)/shard_map/ppermute | solution.py:289
  15.4 2.7 %pairs.1 = f32[1024,128]{1,0:T(8,128)} custom-call(bf16[96,128]{1,0:T(8,128)(2,1)S(1)} %get-tuple-element.10.refs_0_, bf16[96,128]{1,0:T(8,128)(2,1)S(1)} %collective-permute-done.refs_1_, bf16[160,128]{1,0:T(8,128)(2,1)S(1)} %collective-permute-done.1.refs_2_, bf16[192,128]{1,0:T(8,128)(2,1)S(1)} %collective-permute-done.2.refs_3_, ...), custom_call_target="tpu_custom_call" | custom-call | tf_op jit(solution)/shard_map/pairs/pallas_call | solution.py:295
  (22 shorter events, 0.2 us)
Async XLA Ops:
  1.5 5.1 %collective-permute-start = (bf16[96,128]{1,0:T(8,128)(2,1)S(1)}, bf16[96,128]{1,0:T(8,128)(2,1)S(1)}, u32[]{:S(2)}, u32[]{:S(2)}) collective-permute-start(bf16[96,128]{1,0:T(8,128)(2,1)S(1)} %get-tuple-element.11), channel_id=1, source_target_pairs={{0,9},{1,8},{2,11},{3,10},{4,13},{5,12},{6,15},{7,14},{8,1},{9,0},... | collective-permute-start | bytes 73736 | tf_op jit(solution)/shard_map/ppermute | solution.py:289
  6.7 3.6 %collective-permute-start.1 = (bf16[160,128]{1,0:T(8,128)(2,1)S(1)}, bf16[160,128]{1,0:T(8,128)(2,1)S(1)}, u32[]{:S(2)}, u32[]{:S(2)}) collective-permute-start(bf16[160,128]{1,0:T(8,128)(2,1)S(1)} %get-tuple-element.22), channel_id=1, source_target_pairs={{0,5},{1,4},{2,7},{3,6},{4,1},{5,0},{6,3},{7,2},{8,13},{9,12},{10,... | collective-permute-start | bytes 122888 | tf_op jit(solution)/shard_map/ppermute | solution.py:289
  10.4 3.7 %collective-permute-start.2 = (bf16[192,128]{1,0:T(8,128)(2,1)S(1)}, bf16[192,128]{1,0:T(8,128)(2,1)S(1)}, u32[]{:S(2)}, u32[]{:S(2)}) collective-permute-start(bf16[192,128]{1,0:T(8,128)(2,1)S(1)} %get-tuple-element.16), channel_id=1, source_target_pairs={{0,3},{1,2},{2,1},{3,0},{4,7},{5,6},{6,5},{7,4},{8,11},{9,10},{10,... | collective-permute-start | bytes 147464 | tf_op jit(solution)/shard_map/ppermute | solution.py:289
  14.1 1.3 %collective-permute-start.3 = (bf16[256,128]{1,0:T(8,128)(2,1)S(1)}, bf16[256,128]{1,0:T(8,128)(2,1)S(1)}, u32[]{:S(2)}, u32[]{:S(2)}) collective-permute-start(bf16[256,128]{1,0:T(8,128)(2,1)S(1)} %constant_dynamic-update-slice_fusion.19), channel_id=1, source_target_pairs={{0,1},{1,0},{2,3},{3,2},{4,5},{5,4},{6,7},{7,6},{8,9},{9,8},{10,11... | collective-permute-start | bytes 196616 | tf_op jit(solution)/shard_map/ppermute | solution.py:289

commit v3 on v2

--- a/solution.py
+++ b/solution.py
@@ -13,80 +13,65 @@
 VMEM_BYTES = 32 * 1024 * 1024
 
 
-def span(masks):
-    found = [0]
-    for mask in masks:
-        found += [f ^ mask for f in found]
-    return found
-
-
 def distinct(values):
     return sorted(set(values))
 
 
+def reach(stages):
+    found = [0]
+    for masks in stages:
+        found = [f ^ m for m in [0] + masks for f in found]
+    return found
+
+
 class Plan:
-    def __init__(self, masks, split, left_unit, right_unit):
-        self.masks = masks
-        firsts = lambda ms: distinct(m // split for m in span(ms))
-        seconds = lambda ms: distinct(m % split for m in span(ms))
-        self.keep, self.send = [], []
-        rest = masks[1:]
-        left, right = {}, {}
-        at = 0
-        for p in firsts(rest):
-            left[p] = [(0, at)]
-            self.keep.append(("L", p))
-            at += left_unit
-        for p in seconds(rest):
-            right[p] = [(0, at)]
-            self.keep.append(("R", p))
-            at += right_unit
-        self.keep_rows = at
-        v = masks[0]
-        at = 0
-        for p in firsts(rest):
-            left[p].append((1, at))
-            self.send.append(("L", p ^ (v // split)))
-            at += left_unit
-        for p in seconds(rest):
-            right[p].append((1, at))
-            self.send.append(("R", p ^ (v % split)))
-            at += right_unit
-        self.send_rows = at
-        self.messages = []
-        for step in range(1, len(masks)):
-            v, rest = masks[step], masks[step + 1 :]
-            message, at, number = [], 0, step + 1
-            new_left, new_right = {}, {}
-            for p in firsts(rest):
-                new_left[p] = list(left[p])
-                for buffer, row in left[p ^ (v // split)]:
-                    message.append((buffer, row, left_unit))
-                    new_left[p].append((number, at))
-                    at += left_unit
-            for p in seconds(rest):
-                new_right[p] = list(right[p])
-                for buffer, row in right[p ^ (v % split)]:
-                    message.append((buffer, row, right_unit))
-                    new_right[p].append((number, at))
-                    at += right_unit
-            merged = []
-            for buffer, row, count in message:
-                if merged and merged[-1][0] == buffer and merged[-1][1] + merged[-1][2] == row:
-                    merged[-1] = (buffer, merged[-1][1], merged[-1][2] + count)
-                else:
-                    merged.append((buffer, row, count))
-            self.messages.append(merged)
+    def __init__(self, stages, split, left_unit, right_unit):
+        firsts = lambda s: distinct(m // split for m in reach(s))
+        seconds = lambda s: distinct(m % split for m in reach(s))
+        left, right, self.own, self.rows = {}, {}, [], 0
+        for kind, held, positions, unit in (
+            ("L", left, firsts(stages), left_unit),
+            ("R", right, seconds(stages), right_unit),
+        ):
+            for p in positions:
+                held[p] = [(0, self.rows)]
+                self.own.append((kind, p))
+                self.rows += unit
+        self.messages, buffer = [], 0
+        for stage, masks in enumerate(stages):
+            rest = stages[stage + 1 :]
+            new_left = {p: list(left[p]) for p in firsts(rest)}
+            new_right = {p: list(right[p]) for p in seconds(rest)}
+            for mask in masks:
+                buffer += 1
+                message, at = [], 0
+                for new, old, shift, unit in (
+                    (new_left, left, mask // split, left_unit),
+                    (new_right, right, mask % split, right_unit),
+                ):
+                    for p in new:
+                        for source, row in old[p ^ shift]:
+                            if message and message[-1][0] == source and sum(message[-1][1:]) == row:
+                                message[-1] = (source, message[-1][1], message[-1][2] + unit)
+                            else:
+                                message.append((source, row, unit))
+                            new[p].append((buffer, at))
+                            at += unit
+                self.messages.append((stage, mask, message))
             left, right = new_left, new_right
+        self.buffers = buffer + 1
         self.left, self.right = left[0], right[0]
 
 
 def panels_kernel(
     plan, split, x_hbm, tallies_hbm, gain_hbm, offset_hbm, former_hbm, former_bias_hbm, latter_hbm, latter_bias_hbm,
-    matrix_hbm, keep_ref, send_ref, first_ref, second_ref, matrix_ref,
-    x_ref, tallies_ref, gain_ref, offset_ref, former_ref, former_bias_ref, latter_ref, latter_bias_ref,
-    left_ref, right_ref, down_ref, sems,
+    matrix_hbm, *refs,
 ):
+    sends = sum(stage == 0 for stage, _, _ in plan.messages)
+    own_ref, *send_refs = refs[: 1 + sends]
+    first_ref, second_ref, matrix_ref = refs[1 + sends : 4 + sends]
+    x_ref, tallies_ref, gain_ref, offset_ref, former_ref, former_bias_ref, latter_ref, latter_bias_ref = refs[4 + sends : 12 + sends]
+    left_ref, right_ref, down_ref, sems = refs[12 + sends :]
     depth, chain, features = x_ref.shape
     width = former_ref.shape[0]
     first = lax.axis_index("ri")
@@ -153,13 +138,17 @@
             left_ref[block * ROWS : (block + 1) * ROWS] = jnp.concatenate(tiles, 0).astype(jnp.bfloat16)
 
     right_unit = right_ref.shape[0] // split
-    for out_ref, pieces in ((keep_ref, plan.keep), (send_ref, plan.send)):
+    at = 0
+    for kind, position in plan.own:
+        source, index, unit = (left_ref, first, ROWS) if kind == "L" else (right_ref, second, right_unit)
+        start = pl.multiple_of((index ^ position) * unit, ROWS)
+        own_ref[at : at + unit] = source[pl.ds(start, unit)]
+        at += unit
+    for send_ref, (_, _, message) in zip(send_refs, plan.messages):
         at = 0
-        for kind, position in pieces:
-            source, index, unit = (left_ref, first, ROWS) if kind == "L" else (right_ref, second, right_unit)
-            start = pl.multiple_of((index ^ position) * unit, ROWS)
-            out_ref[at : at + unit] = source[pl.ds(start, unit)]
-            at += unit
+        for _, row, count in message:
+            send_ref[at : at + count] = own_ref[row : row + count]
+            at += count
     for out_ref, index in ((first_ref, first), (second_ref, second)):
         count = out_ref.shape[0]
         out_ref[...] = down_ref[pl.ds(pl.multiple_of(index * count, TILE), count)]
@@ -167,8 +156,8 @@
 
 
 def pairs_kernel(plan, first_count, second_count, *refs):
-    buffers = refs[: len(plan.masks) + 1]
-    matrix_ref, first_ref, second_ref, out_ref, gather_ref, left_ref, outer_ref, wide_ref = refs[len(plan.masks) + 1 :]
+    buffers = refs[: plan.buffers]
+    matrix_ref, first_ref, second_ref, out_ref, gather_ref, left_ref, outer_ref, wide_ref = refs[plan.buffers :]
     sources = len(plan.left)
     depth = sources * 2
     width = LANES // 4
@@ -243,12 +232,20 @@
     assert depth == 2 and first_count == TILE and second_count % TILE == 0 and chain % LANES == 0
     left_unit, right_unit = ROWS, ROWS * (second_count // TILE)
     total = size_ri * split
-    masks = []
+    bits = []
     bit = total // 2
-    while bit:
-        masks.append(bit if bit < size_dp else bit | (size_dp // 2))
+    while bit >= size_dp:
+        bits.append(bit)
         bit //= 2
-    plan = Plan(masks, split, left_unit, right_unit)
+    core = size_dp // 2
+    stages = [[bits[0] | core]] if len(bits) % 2 else []
+    bits = bits[len(bits) % 2 :]
+    for high, low in zip(bits[::2], bits[1::2]):
+        stages.append([low | core, high | core, low | high])
+    if core:
+        stages.append([core])
+    plan = Plan(stages, split, left_unit, right_unit)
+    sent = [sum(count for _, _, count in message) for stage, _, message in plan.messages if stage == 0]
 
     vmem = pl.BlockSpec(memory_space=pltpu.VMEM)
     bf16, f32 = jnp.bfloat16, jnp.float32
@@ -263,17 +260,16 @@
         latter_factor_offset[None, :],
     )
     in_hbm = [pltpu.with_memory_space_constraint(a, pltpu.HBM) for a in operands + (pairwise_projection_matrix,)]
-    keep, send, first_tallies, second_tallies, matrix = pl.pallas_call(
+    *own, first_tallies, second_tallies, matrix = pl.pallas_call(
         functools.partial(panels_kernel, plan, split),
         out_shape=(
-            jax.ShapeDtypeStruct((plan.keep_rows, LANES), bf16),
-            jax.ShapeDtypeStruct((plan.send_rows, LANES), bf16),
+            *(jax.ShapeDtypeStruct((rows, LANES), bf16) for rows in [plan.rows] + sent),
             jax.ShapeDtypeStruct((first_count, LANES), f32),
             jax.ShapeDtypeStruct((second_count, LANES), f32),
             jax.ShapeDtypeStruct(pairwise_projection_matrix.shape, f32),
         ),
         in_specs=[pl.BlockSpec(memory_space=pltpu.HBM)] * len(in_hbm),
-        out_specs=(vmem,) * 5,
+        out_specs=(vmem,) * (4 + len(sent)),
         scratch_shapes=[pltpu.VMEM(a.shape, a.dtype) for a in operands]
         + [
             pltpu.VMEM((chain // TILE * ROWS, LANES), bf16),
@@ -287,10 +283,14 @@
 
     axes = ("ri", "rj", "dp")
     swap = lambda v, m: lax.ppermute(v, axes, [(d, d ^ m) for d in range(total)])
-    buffers = [keep, swap(send, masks[0])]
-    for mask, pieces in zip(masks[1:], plan.messages):
-        message = jnp.concatenate([buffers[b][r : r + n] for b, r, n in pieces], 0)
-        buffers.append(swap(message, mask))
+    buffers = own[:1]
+    stage_of = lambda s: [(mask, message) for stage, mask, message in plan.messages if stage == s]
+    for s in range(len(stages)):
+        if s == 0:
+            messages = own[1:]
+        else:
+            messages = [jnp.concatenate([buffers[b][r : r + n] for b, r, n in m], 0) for _, m in stage_of(s)]
+        buffers = buffers + [swap(v, mask) for v, (mask, _) in zip(messages, stage_of(s))]
 
     out = pl.pallas_call(
         functools.partial(pairs_kernel, plan, first_count, second_count),

time: 18.5 us -> 17.5 us (0.946); the launches traced: 18.1 us -> 17.4 us
  starting transfers between devices: 7.74 us -> 7.14 us
    ppermute x4 -> x5, starting transfers between devices: 7.74 us -> 7.14 us  [per_device(): lax.ppermute(v, axes, [(d, d ^ m) for d in range(total)])]
    ppermute x4 -> x5, waiting for transfers between devices: 6.03 us -> 5.92 us  [per_device(): lax.ppermute(v, axes, [(d, d ^ m) for d in range(total)])]
  transfers between devices with their start and end apart: 4 -> 5, of which waited for: 4 -> 3; matrix products, arithmetic and copies ran while one was open for 0% -> 0% of each run, Pallas kernels for 0% -> 0%
where the time goes in v3:
time: 17.5 us; the launch traced here: 17.4 us
  starting transfers between devices  7.14 us (41%)
  waiting for transfers between devices  5.92 us (34%)
  Pallas kernels  4.14 us (24%)
    ppermute x5, starting transfers between devices, per_device(): lax.ppermute(v, axes, [(d, d ^ m) for d in range(total)])  7.14 us
    ppermute x5, waiting for transfers between devices, per_device(): lax.ppermute(v, axes, [(d, d ^ m) for d in range(total)])  5.92 us
    pallas_call x1, Pallas kernels, per_device(): pl.pallas_call(functools.partial(pairs_kernel, plan, first_count, second_...  2.66 us
    pallas_call x1, Pallas kernels, per_device(): pl.pallas_call(functools.partial(panels_kernel, plan, split), out_shape=(...  1.48 us
  transfers between devices with their start and end apart: 5, of which 3 were waited for; matrix products, arithmetic and copies ran while one was open for 0% of the time, Pallas kernels for 0%

profile of v3, /device:TPU:0, one launch (start us, length us, event | category | flops | bytes accessed | tf_op | source)
XLA Modules:
  0.0 17.4 jit_solution(13801852367177273563)
XLA Ops:
  0.0 1.5 %panels.1 = (bf16[128,128]{1,0:T(8,128)(2,1)S(1)}, bf16[96,128]{1,0:T(8,128)(2,1)S(1)}, f32[32,128]{1,0:T(8,128)S(1)}, f32[32,128]{1,0:T(8,128)S(1)}, f32[1024,128]{1,0:T(8,128)S(1)}) custom-call(bf16[2,128,256]{2,1,0:T(8,128)(2,1)} %x_hbm.1, s32[1,128]{1,0:T(1,128)} %bitcast.12, f32[1,256]{1,0:T(1,128)} %bitcast.10, f32[1,256]{1,0:T(1,128)} %bitcast.11, ...), custom_call_target="tpu_custom_call" | custom-call | tf_op jit(solution)/shard_map/panels/pallas_call | solution.py:263
  1.5 3.5 %collective-permute-start = (bf16[96,128]{1,0:T(8,128)(2,1)S(1)}, bf16[96,128]{1,0:T(8,128)(2,1)S(1)}, u32[]{:S(2)}, u32[]{:S(2)}) collective-permute-start(bf16[96,128]{1,0:T(8,128)(2,1)S(1)} %get-tuple-element.11), channel_id=1, source_target_pairs={{0,9},{1,8},{2,11},{3,10},{4,13},{5,12},{6,15},{7,14},{8,1},{9,0},... | collective-permute-start | bytes 73736 | tf_op jit(solution)/shard_map/ppermute | solution.py:285
  5.0 1.6 %collective-permute-done.refs_1_ = bf16[96,128]{1,0:T(8,128)(2,1)S(1)} collective-permute-done((bf16[96,128]{1,0:T(8,128)(2,1)S(1)}, bf16[96,128]{1,0:T(8,128)(2,1)S(1)}, u32[]{:S(2)}, u32[]{:S(2)}) %collective-permute-start) | collective-permute-done | bytes 24608 | tf_op jit(solution)/shard_map/ppermute | solution.py:285
  6.7 1.8 %collective-permute-start.1 = (bf16[96,128]{1,0:T(8,128)(2,1)S(1)}, bf16[96,128]{1,0:T(8,128)(2,1)S(1)}, u32[]{:S(2)}, u32[]{:S(2)}) collective-permute-start(bf16[96,128]{1,0:T(8,128)(2,1)S(1)} %get-tuple-element.26), channel_id=1, source_target_pairs={{0,3},{1,2},{2,1},{3,0},{4,7},{5,6},{6,5},{7,4},{8,11},{9,10},{10,... | collective-permute-start | bytes 73736 | tf_op jit(solution)/shard_map/ppermute | solution.py:285
  8.5 1.5 %collective-permute-start.3 = (bf16[96,128]{1,0:T(8,128)(2,1)S(1)}, bf16[96,128]{1,0:T(8,128)(2,1)S(1)}, u32[]{:S(2)}, u32[]{:S(2)}) collective-permute-start(bf16[96,128]{1,0:T(8,128)(2,1)S(1)} %get-tuple-element.24), channel_id=1, source_target_pairs={{0,6},{1,7},{2,4},{3,5},{4,2},{5,3},{6,0},{7,1},{8,14},{9,15},{10,... | collective-permute-start | bytes 73736 | tf_op jit(solution)/shard_map/ppermute | solution.py:285
  10.1 0.0 collective-permute-start.2
  10.1 0.0 collective-permute-done.1.refs_2_
  10.1 3.2 %collective-permute-done.2.refs_3_ = bf16[96,128]{1,0:T(8,128)(2,1)S(1)} collective-permute-done((bf16[96,128]{1,0:T(8,128)(2,1)S(1)}, bf16[96,128]{1,0:T(8,128)(2,1)S(1)}, u32[]{:S(2)}, u32[]{:S(2)}) %collective-permute-start.2) | collective-permute-done | bytes 24608 | tf_op jit(solution)/shard_map/ppermute | solution.py:285
  13.3 0.0 collective-permute-done.3.refs_4_
  13.4 0.2 %collective-permute-start.4 = (bf16[256,128]{1,0:T(8,128)(2,1)S(1)}, bf16[256,128]{1,0:T(8,128)(2,1)S(1)}, u32[]{:S(2)}, u32[]{:S(2)}) collective-permute-start(bf16[256,128]{1,0:T(8,128)(2,1)S(1)} %constant_dynamic-update-slice_fusion.18), channel_id=1, source_target_pairs={{0,1},{1,0},{2,3},{3,2},{4,5},{5,4},{6,7},{7,6},{8,9},{9,8},{10,11... | collective-permute-start | bytes 196616 | tf_op jit(solution)/shard_map/ppermute | solution.py:285
  13.6 1.1 %collective-permute-done.4.refs_5_ = bf16[256,128]{1,0:T(8,128)(2,1)S(1)} collective-permute-done((bf16[256,128]{1,0:T(8,128)(2,1)S(1)}, bf16[256,128]{1,0:T(8,128)(2,1)S(1)}, u32[]{:S(2)}, u32[]{:S(2)}) %collective-permute-start.4) | collective-permute-done | bytes 65568 | tf_op jit(solution)/shard_map/ppermute | solution.py:285
  14.7 2.7 %pairs.1 = f32[1024,128]{1,0:T(8,128)} custom-call(bf16[128,128]{1,0:T(8,128)(2,1)S(1)} %get-tuple-element.10.refs_0_, bf16[96,128]{1,0:T(8,128)(2,1)S(1)} %collective-permute-done.refs_1_, bf16[96,128]{1,0:T(8,128)(2,1)S(1)} %collective-permute-done.1.refs_2_, bf16[96,128]{1,0:T(8,128)(2,1)S(1)} %collective-permute-done.2.refs_3_, ...), custom_call_target="tpu_custom_call" | custom-call | tf_op jit(solution)/shard_map/pairs/pallas_call | solution.py:295
  (17 shorter events, 0.1 us)
Async XLA Ops:
  1.5 5.1 %collective-permute-start = (bf16[96,128]{1,0:T(8,128)(2,1)S(1)}, bf16[96,128]{1,0:T(8,128)(2,1)S(1)}, u32[]{:S(2)}, u32[]{:S(2)}) collective-permute-start(bf16[96,128]{1,0:T(8,128)(2,1)S(1)} %get-tuple-element.11), channel_id=1, source_target_pairs={{0,9},{1,8},{2,11},{3,10},{4,13},{5,12},{6,15},{7,14},{8,1},{9,0},... | collective-permute-start | bytes 73736 | tf_op jit(solution)/shard_map/ppermute | solution.py:285
  6.7 3.4 %collective-permute-start.1 = (bf16[96,128]{1,0:T(8,128)(2,1)S(1)}, bf16[96,128]{1,0:T(8,128)(2,1)S(1)}, u32[]{:S(2)}, u32[]{:S(2)}) collective-permute-start(bf16[96,128]{1,0:T(8,128)(2,1)S(1)} %get-tuple-element.26), channel_id=1, source_target_pairs={{0,3},{1,2},{2,1},{3,0},{4,7},{5,6},{6,5},{7,4},{8,11},{9,10},{10,... | collective-permute-start | bytes 73736 | tf_op jit(solution)/shard_map/ppermute | solution.py:285
  8.5 4.8 %collective-permute-start.3 = (bf16[96,128]{1,0:T(8,128)(2,1)S(1)}, bf16[96,128]{1,0:T(8,128)(2,1)S(1)}, u32[]{:S(2)}, u32[]{:S(2)}) collective-permute-start(bf16[96,128]{1,0:T(8,128)(2,1)S(1)} %get-tuple-element.24), channel_id=1, source_target_pairs={{0,6},{1,7},{2,4},{3,5},{4,2},{5,3},{6,0},{7,1},{8,14},{9,15},{10,... | collective-permute-start | bytes 73736 | tf_op jit(solution)/shard_map/ppermute | solution.py:285
  10.1 3.3 %collective-permute-start.2 = (bf16[96,128]{1,0:T(8,128)(2,1)S(1)}, bf16[96,128]{1,0:T(8,128)(2,1)S(1)}, u32[]{:S(2)}, u32[]{:S(2)}) collective-permute-start(bf16[96,128]{1,0:T(8,128)(2,1)S(1)} %get-tuple-element.25), channel_id=1, source_target_pairs={{0,5},{1,4},{2,7},{3,6},{4,1},{5,0},{6,3},{7,2},{8,13},{9,12},{10,... | collective-permute-start | bytes 73736 | tf_op jit(solution)/shard_map/ppermute | solution.py:285
  13.4 1.3 %collective-permute-start.4 = (bf16[256,128]{1,0:T(8,128)(2,1)S(1)}, bf16[256,128]{1,0:T(8,128)(2,1)S(1)}, u32[]{:S(2)}, u32[]{:S(2)}) collective-permute-start(bf16[256,128]{1,0:T(8,128)(2,1)S(1)} %constant_dynamic-update-slice_fusion.18), channel_id=1, source_target_pairs={{0,1},{1,0},{2,3},{3,2},{4,5},{5,4},{6,7},{7,6},{8,9},{9,8},{10,11... | collective-permute-start | bytes 196616 | tf_op jit(solution)/shard_map/ppermute | solution.py:285

commit v4 on v3

--- a/solution.py
+++ b/solution.py
@@ -151,13 +151,15 @@
             at += count
     for out_ref, index in ((first_ref, first), (second_ref, second)):
         count = out_ref.shape[0]
-        out_ref[...] = down_ref[pl.ds(pl.multiple_of(index * count, TILE), count)]
+        out_ref[...] = 1.0 / (down_ref[pl.ds(pl.multiple_of(index * count, TILE), count)] + 0.001)
     matrix_copy.wait()
 
 
-def pairs_kernel(plan, first_count, second_count, *refs):
+def pairs_kernel(plan, *refs):
     buffers = refs[: plan.buffers]
-    matrix_ref, first_ref, second_ref, out_ref, gather_ref, left_ref, outer_ref, wide_ref = refs[plan.buffers :]
+    matrix_ref, first_ref, second_ref, out_ref = refs[plan.buffers : plan.buffers + 4]
+    gather_ref, left_ref, outer_ref, wide_ref, done_ref, sems = refs[plan.buffers + 4 :]
+    first_count, second_count, _ = out_ref.shape
     sources = len(plan.left)
     depth = sources * 2
     width = LANES // 4
@@ -171,27 +173,33 @@
     high = matrix.astype(jnp.bfloat16)
     wide_ref[:, :LANES] = high
     wide_ref[:, LANES:] = (matrix - high.astype(jnp.float32)).astype(jnp.bfloat16)
-    first_tallies = first_ref[...]
+    first_scale = first_ref[...]
 
     def one_block(block, carry):
         for k, (buffer, row) in enumerate(plan.right):
             start = pl.multiple_of(row + block * ROWS, ROWS)
-            gather_ref[k * ROWS : (k + 1) * ROWS] = buffers[buffer][pl.ds(start, ROWS)].astype(jnp.float32)
+            at = (sources + k) * ROWS
+            gather_ref[at : at + ROWS] = buffers[buffer][pl.ds(start, ROWS)].astype(jnp.float32)
         left = left_ref[...]
         lane_block = lax.broadcasted_iota(jnp.int32, (depth, LANES), 1) // width
+        zero = jnp.zeros((depth, LANES), jnp.bfloat16)
+        turned = []
         for j8 in range(8):
-            plain = gather_ref[pl.ds(j8, depth, stride=8)]
-            turned = [plain] + [pltpu.roll(plain, r * width, 1) for r in range(1, 4)]
-            for pair in range(2):
-                columns = []
-                for q in (2 * pair, 2 * pair + 1):
-                    columns.append(
-                        jnp.concatenate([jnp.where(lane_block == c, turned[(c - q) % 4], 0.0) for c in range(4)], 0)
-                    )
-                spread = jnp.concatenate(columns, 1).astype(jnp.bfloat16)
+            plain = gather_ref[pl.ds(sources * ROWS + j8, depth, stride=8)]
+            turned.append([(pltpu.roll(plain, r * width, 1) if r else plain).astype(jnp.bfloat16) for r in range(4)])
+
+        def outer(q):
+            for j8 in range(0, 8, 2):
+                spread = jnp.concatenate(
+                    [
+                        jnp.concatenate([jnp.where(lane_block == c, t[(c - q) % 4], zero) for c in range(4)], 0)
+                        for t in turned[j8 : j8 + 2]
+                    ],
+                    1,
+                )
                 product = jnp.dot(left, spread, preferred_element_type=jnp.float32).astype(jnp.bfloat16)
-                for at, q in enumerate((2 * pair, 2 * pair + 1)):
-                    j = q * 8 + j8
+                for at in range(2):
+                    j = q * 8 + j8 + at
                     for half in range(2):
                         for gq in range(4):
                             rows = (half * 4 + gq) * TILE
@@ -199,12 +207,29 @@
                             outer_ref[j * TILE : (j + 1) * TILE, group * LANES : (group + 1) * LANES] = (
                                 product[rows : rows + TILE, at * LANES : (at + 1) * LANES]
                             )
-        projected = jnp.dot(outer_ref[...], wide_ref[...], preferred_element_type=jnp.float32)
-        projected = projected[:, :LANES] + projected[:, LANES:]
-        for j in range(TILE):
-            at = block * TILE + j
-            bound = jnp.minimum(first_tallies, second_ref[pl.ds(at, 1)]) + 0.001
-            out_ref[pl.ds(at, first_count, stride=second_count)] = projected[j * TILE : (j + 1) * TILE] / bound
+
+        def project(q):
+            rows = outer_ref[q * 8 * TILE : (q + 1) * 8 * TILE]
+            projected = jnp.dot(rows, wide_ref[...], preferred_element_type=jnp.float32)
+            projected = projected[:, :LANES] + projected[:, LANES:]
+            start = pl.multiple_of(block * TILE + q * 8, 8)
+            for k in range(8):
+                scale = jnp.maximum(first_scale, second_ref[pl.ds(start + k, 1)])
+                done_ref[q, pl.ds(k, first_count, stride=8)] = projected[k * TILE : (k + 1) * TILE] * scale
+            return pltpu.make_async_copy(
+                done_ref.at[q].reshape(first_count, 8, LANES), out_ref.at[:, pl.ds(start, 8)], sems.at[q]
+            )
+
+        outer(0)
+        outer(1)
+        copies = []
+        for q in range(4):
+            if q + 2 < 4:
+                outer(q + 2)
+            copies.append(project(q))
+            copies[-1].start()
+        for copy in copies:
+            copy.wait()
         return carry
 
     blocks = second_count // TILE
@@ -260,7 +285,7 @@
         latter_factor_offset[None, :],
     )
     in_hbm = [pltpu.with_memory_space_constraint(a, pltpu.HBM) for a in operands + (pairwise_projection_matrix,)]
-    *own, first_tallies, second_tallies, matrix = pl.pallas_call(
+    *own, first_scale, second_scale, matrix = pl.pallas_call(
         functools.partial(panels_kernel, plan, split),
         out_shape=(
             *(jax.ShapeDtypeStruct((rows, LANES), bf16) for rows in [plan.rows] + sent),
@@ -292,21 +317,22 @@
             messages = [jnp.concatenate([buffers[b][r : r + n] for b, r, n in m], 0) for _, m in stage_of(s)]
         buffers = buffers + [swap(v, mask) for v, (mask, _) in zip(messages, stage_of(s))]
 
-    out = pl.pallas_call(
-        functools.partial(pairs_kernel, plan, first_count, second_count),
-        out_shape=jax.ShapeDtypeStruct((first_count * second_count, LANES), f32),
+    return pl.pallas_call(
+        functools.partial(pairs_kernel, plan),
+        out_shape=jax.ShapeDtypeStruct((first_count, second_count, LANES), f32),
         in_specs=[vmem] * (len(buffers) + 3),
-        out_specs=vmem,
+        out_specs=pl.BlockSpec(memory_space=pl.ANY),
         scratch_shapes=[
-            pltpu.VMEM((total * ROWS, LANES), f32),
+            pltpu.VMEM((2 * total * ROWS, LANES), f32),
             pltpu.VMEM((2 * LANES, 4 * total * 2), bf16),
             pltpu.VMEM((first_count * TILE, 8 * LANES), bf16),
             pltpu.VMEM((8 * LANES, 2 * LANES), bf16),
+            pltpu.VMEM((4, first_count * 8, LANES), f32),
+            pltpu.SemaphoreType.DMA((4,)),
         ],
         compiler_params=pltpu.CompilerParams(vmem_limit_bytes=VMEM_BYTES),
         name="pairs",
-    )(*buffers, matrix, first_tallies, second_tallies)
-    return out.reshape(first_count, second_count, LANES)
+    )(*buffers, matrix, first_scale, second_scale)
 
 
 def solution(mesh):

time: 17.5 us -> 17 us (0.971)
  Pallas kernels: 4.14 us -> 3.59 us
    pallas_call x1, Pallas kernels: 2.66 us -> 2.12 us  [per_device(): pl.pallas_call(functools.partial(pairs_kernel, plan), out_shape=jax.Shape...]
where the time goes in v4:
time: 17 us; the launch traced here: 16.8 us
  starting transfers between devices  7.14 us (42%)
  waiting for transfers between devices  5.92 us (35%)
  Pallas kernels  3.59 us (21%)
    ppermute x5, starting transfers between devices, per_device(): lax.ppermute(v, axes, [(d, d ^ m) for d in range(total)])  7.14 us
    ppermute x5, waiting for transfers between devices, per_device(): lax.ppermute(v, axes, [(d, d ^ m) for d in range(total)])  5.92 us
    pallas_call x1, Pallas kernels, per_device(): pl.pallas_call(functools.partial(pairs_kernel, plan), out_shape=jax.Shape...  2.12 us
    pallas_call x1, Pallas kernels, per_device(): pl.pallas_call(functools.partial(panels_kernel, plan, split), out_shape=(...  1.48 us
  transfers between devices with their start and end apart: 5, of which 3 were waited for; matrix products, arithmetic and copies ran while one was open for 0% of the time, Pallas kernels for 0%

profile of v4, /device:TPU:0, one launch (start us, length us, event | category | flops | bytes accessed | tf_op | source)
XLA Modules:
  0.0 16.8 jit_solution(13979385162868697496)
XLA Ops:
  0.0 1.5 %panels.1 = (bf16[128,128]{1,0:T(8,128)(2,1)S(1)}, bf16[96,128]{1,0:T(8,128)(2,1)S(1)}, f32[32,128]{1,0:T(8,128)S(1)}, f32[32,128]{1,0:T(8,128)S(1)}, f32[1024,128]{1,0:T(8,128)S(1)}) custom-call(bf16[2,128,256]{2,1,0:T(8,128)(2,1)} %x_hbm.1, s32[1,128]{1,0:T(1,128)} %bitcast.11, f32[1,256]{1,0:T(1,128)} %bitcast.9, f32[1,256]{1,0:T(1,128)} %bitcast.10, ...), custom_call_target="tpu_custom_call" | custom-call | tf_op jit(solution)/shard_map/panels/pallas_call | solution.py:288
  1.5 3.5 %collective-permute-start = (bf16[96,128]{1,0:T(8,128)(2,1)S(1)}, bf16[96,128]{1,0:T(8,128)(2,1)S(1)}, u32[]{:S(2)}, u32[]{:S(2)}) collective-permute-start(bf16[96,128]{1,0:T(8,128)(2,1)S(1)} %get-tuple-element.11), channel_id=1, source_target_pairs={{0,9},{1,8},{2,11},{3,10},{4,13},{5,12},{6,15},{7,14},{8,1},{9,0},... | collective-permute-start | bytes 73736 | tf_op jit(solution)/shard_map/ppermute | solution.py:310
  5.0 1.6 %collective-permute-done.refs_1_ = bf16[96,128]{1,0:T(8,128)(2,1)S(1)} collective-permute-done((bf16[96,128]{1,0:T(8,128)(2,1)S(1)}, bf16[96,128]{1,0:T(8,128)(2,1)S(1)}, u32[]{:S(2)}, u32[]{:S(2)}) %collective-permute-start) | collective-permute-done | bytes 24608 | tf_op jit(solution)/shard_map/ppermute | solution.py:310
  6.7 1.8 %collective-permute-start.1 = (bf16[96,128]{1,0:T(8,128)(2,1)S(1)}, bf16[96,128]{1,0:T(8,128)(2,1)S(1)}, u32[]{:S(2)}, u32[]{:S(2)}) collective-permute-start(bf16[96,128]{1,0:T(8,128)(2,1)S(1)} %get-tuple-element.26), channel_id=1, source_target_pairs={{0,3},{1,2},{2,1},{3,0},{4,7},{5,6},{6,5},{7,4},{8,11},{9,10},{10,... | collective-permute-start | bytes 73736 | tf_op jit(solution)/shard_map/ppermute | solution.py:310
  8.5 1.5 %collective-permute-start.3 = (bf16[96,128]{1,0:T(8,128)(2,1)S(1)}, bf16[96,128]{1,0:T(8,128)(2,1)S(1)}, u32[]{:S(2)}, u32[]{:S(2)}) collective-permute-start(bf16[96,128]{1,0:T(8,128)(2,1)S(1)} %get-tuple-element.24), channel_id=1, source_target_pairs={{0,6},{1,7},{2,4},{3,5},{4,2},{5,3},{6,0},{7,1},{8,14},{9,15},{10,... | collective-permute-start | bytes 73736 | tf_op jit(solution)/shard_map/ppermute | solution.py:310
  10.1 0.0 collective-permute-start.2
  10.1 0.0 collective-permute-done.1.refs_2_
  10.1 3.2 %collective-permute-done.2.refs_3_ = bf16[96,128]{1,0:T(8,128)(2,1)S(1)} collective-permute-done((bf16[96,128]{1,0:T(8,128)(2,1)S(1)}, bf16[96,128]{1,0:T(8,128)(2,1)S(1)}, u32[]{:S(2)}, u32[]{:S(2)}) %collective-permute-start.2) | collective-permute-done | bytes 24608 | tf_op jit(solution)/shard_map/ppermute | solution.py:310
  13.3 0.0 collective-permute-done.3.refs_4_
  13.4 0.2 %collective-permute-start.4 = (bf16[256,128]{1,0:T(8,128)(2,1)S(1)}, bf16[256,128]{1,0:T(8,128)(2,1)S(1)}, u32[]{:S(2)}, u32[]{:S(2)}) collective-permute-start(bf16[256,128]{1,0:T(8,128)(2,1)S(1)} %constant_dynamic-update-slice_fusion.18), channel_id=1, source_target_pairs={{0,1},{1,0},{2,3},{3,2},{4,5},{5,4},{6,7},{7,6},{8,9},{9,8},{10,11... | collective-permute-start | bytes 196616 | tf_op jit(solution)/shard_map/ppermute | solution.py:310
  13.6 1.1 %collective-permute-done.4.refs_5_ = bf16[256,128]{1,0:T(8,128)(2,1)S(1)} collective-permute-done((bf16[256,128]{1,0:T(8,128)(2,1)S(1)}, bf16[256,128]{1,0:T(8,128)(2,1)S(1)}, u32[]{:S(2)}, u32[]{:S(2)}) %collective-permute-start.4) | collective-permute-done | bytes 65568 | tf_op jit(solution)/shard_map/ppermute | solution.py:310
  14.7 2.1 %pairs.1 = f32[32,32,128]{2,1,0:T(8,128)} custom-call(bf16[128,128]{1,0:T(8,128)(2,1)S(1)} %get-tuple-element.10.refs_0_, bf16[96,128]{1,0:T(8,128)(2,1)S(1)} %collective-permute-done.refs_1_, bf16[96,128]{1,0:T(8,128)(2,1)S(1)} %collective-permute-done.1.refs_2_, bf16[96,128]{1,0:T(8,128)(2,1)S(1)} %collective-permute-done.2.refs_3_, ...), custom_call_target="tpu_custom_call" | custom-call | tf_op jit(solution)/shard_map/pairs/pallas_call | solution.py:320
  (17 shorter events, 0.1 us)
Async XLA Ops:
  1.5 5.1 %collective-permute-start = (bf16[96,128]{1,0:T(8,128)(2,1)S(1)}, bf16[96,128]{1,0:T(8,128)(2,1)S(1)}, u32[]{:S(2)}, u32[]{:S(2)}) collective-permute-start(bf16[96,128]{1,0:T(8,128)(2,1)S(1)} %get-tuple-element.11), channel_id=1, source_target_pairs={{0,9},{1,8},{2,11},{3,10},{4,13},{5,12},{6,15},{7,14},{8,1},{9,0},... | collective-permute-start | bytes 73736 | tf_op jit(solution)/shard_map/ppermute | solution.py:310
  6.7 3.4 %collective-permute-start.1 = (bf16[96,128]{1,0:T(8,128)(2,1)S(1)}, bf16[96,128]{1,0:T(8,128)(2,1)S(1)}, u32[]{:S(2)}, u32[]{:S(2)}) collective-permute-start(bf16[96,128]{1,0:T(8,128)(2,1)S(1)} %get-tuple-element.26), channel_id=1, source_target_pairs={{0,3},{1,2},{2,1},{3,0},{4,7},{5,6},{6,5},{7,4},{8,11},{9,10},{10,... | collective-permute-start | bytes 73736 | tf_op jit(solution)/shard_map/ppermute | solution.py:310
  8.5 4.8 %collective-permute-start.3 = (bf16[96,128]{1,0:T(8,128)(2,1)S(1)}, bf16[96,128]{1,0:T(8,128)(2,1)S(1)}, u32[]{:S(2)}, u32[]{:S(2)}) collective-permute-start(bf16[96,128]{1,0:T(8,128)(2,1)S(1)} %get-tuple-element.24), channel_id=1, source_target_pairs={{0,6},{1,7},{2,4},{3,5},{4,2},{5,3},{6,0},{7,1},{8,14},{9,15},{10,... | collective-permute-start | bytes 73736 | tf_op jit(solution)/shard_map/ppermute | solution.py:310
  10.1 3.3 %collective-permute-start.2 = (bf16[96,128]{1,0:T(8,128)(2,1)S(1)}, bf16[96,128]{1,0:T(8,128)(2,1)S(1)}, u32[]{:S(2)}, u32[]{:S(2)}) collective-permute-start(bf16[96,128]{1,0:T(8,128)(2,1)S(1)} %get-tuple-element.25), channel_id=1, source_target_pairs={{0,5},{1,4},{2,7},{3,6},{4,1},{5,0},{6,3},{7,2},{8,13},{9,12},{10,... | collective-permute-start | bytes 73736 | tf_op jit(solution)/shard_map/ppermute | solution.py:310
  13.4 1.3 %collective-permute-start.4 = (bf16[256,128]{1,0:T(8,128)(2,1)S(1)}, bf16[256,128]{1,0:T(8,128)(2,1)S(1)}, u32[]{:S(2)}, u32[]{:S(2)}) collective-permute-start(bf16[256,128]{1,0:T(8,128)(2,1)S(1)} %constant_dynamic-update-slice_fusion.18), channel_id=1, source_target_pairs={{0,1},{1,0},{2,3},{3,2},{4,5},{5,4},{6,7},{7,6},{8,9},{9,8},{10,11... | collective-permute-start | bytes 196616 | tf_op jit(solution)/shard_map/ppermute | solution.py:310

commit v5 on v4

--- a/solution.py
+++ b/solution.py
@@ -266,7 +266,7 @@
     stages = [[bits[0] | core]] if len(bits) % 2 else []
     bits = bits[len(bits) % 2 :]
     for high, low in zip(bits[::2], bits[1::2]):
-        stages.append([low | core, high | core, low | high])
+        stages.append([low | core, high | core, low | high | core])
     if core:
         stages.append([core])
     plan = Plan(stages, split, left_unit, right_unit)
@@ -307,15 +307,32 @@
     )(*in_hbm)
 
     axes = ("ri", "rj", "dp")
-    swap = lambda v, m: lax.ppermute(v, axes, [(d, d ^ m) for d in range(total)])
+    me = lax.axis_index(axes)
+    move = lambda v, mask_of: lax.ppermute(v, axes, [(d, d ^ mask_of(d)) for d in range(total)])
     buffers = own[:1]
-    stage_of = lambda s: [(mask, message) for stage, mask, message in plan.messages if stage == s]
-    for s in range(len(stages)):
+    for s, masks in enumerate(stages):
         if s == 0:
             messages = own[1:]
         else:
-            messages = [jnp.concatenate([buffers[b][r : r + n] for b, r, n in m], 0) for _, m in stage_of(s)]
-        buffers = buffers + [swap(v, mask) for v, (mask, _) in zip(messages, stage_of(s))]
+            messages = [
+                jnp.concatenate([buffers[b][r : r + n] for b, r, n in message], 0)
+                for stage, _, message in plan.messages
+                if stage == s
+            ]
+        if len(masks) == 3:
+            one, two, across = masks
+            low, high = one & ~core, two & ~core
+            even = lambda d: ((d & low) != 0) == ((d & high) != 0)
+            messages = [
+                jnp.where(even(me), messages[1], messages[0]),
+                jnp.where(even(me), messages[0], messages[1]),
+                messages[2],
+            ]
+            messages = list(lax.optimization_barrier(tuple(messages)))
+            ways = [lambda d: two if even(d) else one, lambda d: one if even(d) else two, lambda d: across]
+        else:
+            ways = [lambda d: masks[0]]
+        buffers = buffers + [move(v, way) for v, way in zip(messages, ways)]
 
     return pl.pallas_call(
         functools.partial(pairs_kernel, plan),

time: 17 us -> 16.5 us (0.971)
  waiting for transfers between devices: 5.92 us -> 4.01 us
  starting transfers between devices: 7.14 us -> 8.62 us
    ppermute x5, waiting for transfers between devices: 5.92 us -> 4.01 us  [per_device(): lax.ppermute(v, axes, [(d, d ^ mask_of(d)) for d in range(total)])]
    ppermute x5, starting transfers between devices: 7.14 us -> 8.62 us  [per_device(): lax.ppermute(v, axes, [(d, d ^ mask_of(d)) for d in range(total)])]
  transfers between devices with their start and end apart: 5 -> 5, of which waited for: 3 -> 4; matrix products, arithmetic and copies ran while one was open for 0% -> 0% of each run, Pallas kernels for 0% -> 0%
where the time goes in v5:
time: 16.5 us; the launch traced here: 16.4 us
  starting transfers between devices  8.62 us (52%)
  waiting for transfers between devices  4.01 us (24%)
  Pallas kernels  3.59 us (22%)
    ppermute x5, starting transfers between devices, per_device(): lax.ppermute(v, axes, [(d, d ^ mask_of(d)) for d in range(total)])  8.62 us
    ppermute x5, waiting for transfers between devices, per_device(): lax.ppermute(v, axes, [(d, d ^ mask_of(d)) for d in range(total)])  4.01 us
    pallas_call x1, Pallas kernels, per_device(): pl.pallas_call(functools.partial(pairs_kernel, plan), out_shape=jax.Shape...  2.12 us
    pallas_call x1, Pallas kernels, per_device(): pl.pallas_call(functools.partial(panels_kernel, plan, split), out_shape=(...  1.48 us
  transfers between devices with their start and end apart: 5, of which 4 were waited for; matrix products, arithmetic and copies ran while one was open for 0% of the time, Pallas kernels for 0%

profile of v5, /device:TPU:0, one launch (start us, length us, event | category | flops | bytes accessed | tf_op | source)
XLA Modules:
  0.0 16.4 jit_solution(15349361914662890386)
XLA Ops:
  0.0 1.5 %panels.1 = (bf16[128,128]{1,0:T(8,128)(2,1)S(1)}, bf16[96,128]{1,0:T(8,128)(2,1)S(1)}, f32[32,128]{1,0:T(8,128)S(1)}, f32[32,128]{1,0:T(8,128)S(1)}, f32[1024,128]{1,0:T(8,128)S(1)}) custom-call(bf16[2,128,256]{2,1,0:T(8,128)(2,1)} %x_hbm.1, s32[1,128]{1,0:T(1,128)} %bitcast.11, f32[1,256]{1,0:T(1,128)} %bitcast.9, f32[1,256]{1,0:T(1,128)} %bitcast.10, ...), custom_call_target="tpu_custom_call" | custom-call | tf_op jit(solution)/shard_map/panels/pallas_call | solution.py:288
  1.5 3.5 %collective-permute-start = (bf16[96,128]{1,0:T(8,128)(2,1)S(1)}, bf16[96,128]{1,0:T(8,128)(2,1)S(1)}, u32[]{:S(2)}, u32[]{:S(2)}) collective-permute-start(bf16[96,128]{1,0:T(8,128)(2,1)S(1)} %get-tuple-element.14), channel_id=1, source_target_pairs={{0,9},{1,8},{2,11},{3,10},{4,13},{5,12},{6,15},{7,14},{8,1},{9,0},... | collective-permute-start | bytes 73736 | tf_op jit(solution)/shard_map/ppermute | solution.py:311
  5.0 1.6 %collective-permute-done.refs_1_ = bf16[96,128]{1,0:T(8,128)(2,1)S(1)} collective-permute-done((bf16[96,128]{1,0:T(8,128)(2,1)S(1)}, bf16[96,128]{1,0:T(8,128)(2,1)S(1)}, u32[]{:S(2)}, u32[]{:S(2)}) %collective-permute-start) | collective-permute-done | bytes 24608 | tf_op jit(solution)/shard_map/ppermute | solution.py:311
  6.7 1.9 %collective-permute-start.1 = (bf16[96,128]{1,0:T(8,128)(2,1)S(1)}, bf16[96,128]{1,0:T(8,128)(2,1)S(1)}, u32[]{:S(2)}, u32[]{:S(2)}) collective-permute-start(bf16[96,128]{1,0:T(8,128)(2,1)S(1)} %get-tuple-element.15), channel_id=1, source_target_pairs={{0,5},{1,4},{2,1},{3,0},{4,7},{5,6},{6,3},{7,2},{8,13},{9,12},{10,... | collective-permute-start | bytes 73736 | tf_op jit(solution)/shard_map/ppermute | solution.py:311
  8.6 0.0 collective-permute-start.2
  8.6 2.7 %collective-permute-start.3 = (bf16[96,128]{1,0:T(8,128)(2,1)S(1)}, bf16[96,128]{1,0:T(8,128)(2,1)S(1)}, u32[]{:S(2)}, u32[]{:S(2)}) collective-permute-start(bf16[96,128]{1,0:T(8,128)(2,1)S(1)} %constant_dynamic-update-slice_fusion.12), channel_id=1, source_target_pairs={{0,7},{1,6},{2,5},{3,4},{4,3},{5,2},{6,1},{7,0},{8,15},{9,14},{10,... | collective-permute-start | bytes 73736 | tf_op jit(solution)/shard_map/ppermute | solution.py:311
  11.3 0.0 collective-permute-done.1.refs_2_
  11.3 0.6 %collective-permute-done.2.refs_3_ = bf16[96,128]{1,0:T(8,128)(2,1)S(1)} collective-permute-done((bf16[96,128]{1,0:T(8,128)(2,1)S(1)}, bf16[96,128]{1,0:T(8,128)(2,1)S(1)}, u32[]{:S(2)}, u32[]{:S(2)}) %collective-permute-start.2) | collective-permute-done | bytes 24608 | tf_op jit(solution)/shard_map/ppermute | solution.py:311
  11.9 0.9 %collective-permute-done.3.refs_4_ = bf16[96,128]{1,0:T(8,128)(2,1)S(1)} collective-permute-done((bf16[96,128]{1,0:T(8,128)(2,1)S(1)}, bf16[96,128]{1,0:T(8,128)(2,1)S(1)}, u32[]{:S(2)}, u32[]{:S(2)}) %collective-permute-start.3) | collective-permute-done | bytes 24608 | tf_op jit(solution)/shard_map/ppermute | solution.py:311
  12.9 0.5 %collective-permute-start.4 = (bf16[256,128]{1,0:T(8,128)(2,1)S(1)}, bf16[256,128]{1,0:T(8,128)(2,1)S(1)}, u32[]{:S(2)}, u32[]{:S(2)}) collective-permute-start(bf16[256,128]{1,0:T(8,128)(2,1)S(1)} %constant_dynamic-update-slice_fusion.18), channel_id=1, source_target_pairs={{0,1},{1,0},{2,3},{3,2},{4,5},{5,4},{6,7},{7,6},{8,9},{9,8},{10,11... | collective-permute-start | bytes 196616 | tf_op jit(solution)/shard_map/ppermute | solution.py:311
  13.4 0.9 %collective-permute-done.4.refs_5_ = bf16[256,128]{1,0:T(8,128)(2,1)S(1)} collective-permute-done((bf16[256,128]{1,0:T(8,128)(2,1)S(1)}, bf16[256,128]{1,0:T(8,128)(2,1)S(1)}, u32[]{:S(2)}, u32[]{:S(2)}) %collective-permute-start.4) | collective-permute-done | bytes 65568 | tf_op jit(solution)/shard_map/ppermute | solution.py:311
  14.3 2.1 %pairs.1 = f32[32,32,128]{2,1,0:T(8,128)} custom-call(bf16[128,128]{1,0:T(8,128)(2,1)S(1)} %get-tuple-element.13.refs_0_, bf16[96,128]{1,0:T(8,128)(2,1)S(1)} %collective-permute-done.refs_1_, bf16[96,128]{1,0:T(8,128)(2,1)S(1)} %collective-permute-done.1.refs_2_, bf16[96,128]{1,0:T(8,128)(2,1)S(1)} %collective-permute-done.2.refs_3_, ...), custom_call_target="tpu_custom_call" | custom-call | tf_op jit(solution)/shard_map/pairs/pallas_call | solution.py:337
  (18 shorter events, 0.1 us)
Async XLA Ops:
  1.5 5.1 %collective-permute-start = (bf16[96,128]{1,0:T(8,128)(2,1)S(1)}, bf16[96,128]{1,0:T(8,128)(2,1)S(1)}, u32[]{:S(2)}, u32[]{:S(2)}) collective-permute-start(bf16[96,128]{1,0:T(8,128)(2,1)S(1)} %get-tuple-element.14), channel_id=1, source_target_pairs={{0,9},{1,8},{2,11},{3,10},{4,13},{5,12},{6,15},{7,14},{8,1},{9,0},... | collective-permute-start | bytes 73736 | tf_op jit(solution)/shard_map/ppermute | solution.py:311
  6.7 4.6 %collective-permute-start.1 = (bf16[96,128]{1,0:T(8,128)(2,1)S(1)}, bf16[96,128]{1,0:T(8,128)(2,1)S(1)}, u32[]{:S(2)}, u32[]{:S(2)}) collective-permute-start(bf16[96,128]{1,0:T(8,128)(2,1)S(1)} %get-tuple-element.15), channel_id=1, source_target_pairs={{0,5},{1,4},{2,1},{3,0},{4,7},{5,6},{6,3},{7,2},{8,13},{9,12},{10,... | collective-permute-start | bytes 73736 | tf_op jit(solution)/shard_map/ppermute | solution.py:311
  8.6 3.3 %collective-permute-start.2 = (bf16[96,128]{1,0:T(8,128)(2,1)S(1)}, bf16[96,128]{1,0:T(8,128)(2,1)S(1)}, u32[]{:S(2)}, u32[]{:S(2)}) collective-permute-start(bf16[96,128]{1,0:T(8,128)(2,1)S(1)} %get-tuple-element.16), channel_id=1, source_target_pairs={{0,3},{1,2},{2,7},{3,6},{4,1},{5,0},{6,5},{7,4},{8,11},{9,10},{10,... | collective-permute-start | bytes 73736 | tf_op jit(solution)/shard_map/ppermute | solution.py:311
  8.6 4.2 %collective-permute-start.3 = (bf16[96,128]{1,0:T(8,128)(2,1)S(1)}, bf16[96,128]{1,0:T(8,128)(2,1)S(1)}, u32[]{:S(2)}, u32[]{:S(2)}) collective-permute-start(bf16[96,128]{1,0:T(8,128)(2,1)S(1)} %constant_dynamic-update-slice_fusion.12), channel_id=1, source_target_pairs={{0,7},{1,6},{2,5},{3,4},{4,3},{5,2},{6,1},{7,0},{8,15},{9,14},{10,... | collective-permute-start | bytes 73736 | tf_op jit(solution)/shard_map/ppermute | solution.py:311
  12.9 1.4 %collective-permute-start.4 = (bf16[256,128]{1,0:T(8,128)(2,1)S(1)}, bf16[256,128]{1,0:T(8,128)(2,1)S(1)}, u32[]{:S(2)}, u32[]{:S(2)}) collective-permute-start(bf16[256,128]{1,0:T(8,128)(2,1)S(1)} %constant_dynamic-update-slice_fusion.18), channel_id=1, source_target_pairs={{0,1},{1,0},{2,3},{3,2},{4,5},{5,4},{6,7},{7,6},{8,9},{9,8},{10,11... | collective-permute-start | bytes 196616 | tf_op jit(solution)/shard_map/ppermute | solution.py:311

commit v6 on v5

--- a/solution.py
+++ b/solution.py
@@ -155,45 +155,79 @@
     matrix_copy.wait()
 
 
-def pairs_kernel(plan, *refs):
-    buffers = refs[: plan.buffers]
-    matrix_ref, first_ref, second_ref, out_ref = refs[plan.buffers : plan.buffers + 4]
-    gather_ref, left_ref, outer_ref, wide_ref, done_ref, sems = refs[plan.buffers + 4 :]
-    first_count, second_count, _ = out_ref.shape
-    sources = len(plan.left)
+def gathered(scratch_ref, buffers, tiles, block):
+    for k, (buffer, row) in enumerate(tiles):
+        start = pl.multiple_of(row + block * ROWS, ROWS)
+        scratch_ref[k * ROWS : (k + 1) * ROWS] = buffers[buffer][pl.ds(start, ROWS)].astype(jnp.float32)
+
+
+def stacked(scratch_ref, half, depth):
+    return jnp.concatenate([scratch_ref[pl.ds(half * 4 + c, depth, stride=8)] for c in range(4)], 0)
+
+
+def turns(scratch_ref, j8, depth):
+    plain = scratch_ref[pl.ds(j8, depth, stride=8)]
+    return [(pltpu.roll(plain, r * LANES // 4, 1) if r else plain).astype(jnp.bfloat16) for r in range(4)]
+
+
+def ready_kernel(plan, blocks, *refs):
+    buffers = refs[: plan.buffers - 1]
+    matrix_ref, wide_ref, stack_ref, turned_ref, gather_ref = refs[plan.buffers - 1 :]
+    sources = len(plan.left) // 2
     depth = sources * 2
-    width = LANES // 4
-
-    for k, (buffer, row) in enumerate(plan.left):
-        gather_ref[k * ROWS : (k + 1) * ROWS] = buffers[buffer][row : row + ROWS].astype(jnp.float32)
+    gathered(gather_ref, buffers, plan.left[:sources], 0)
     for half in range(2):
-        stacked = jnp.concatenate([gather_ref[pl.ds(half * 4 + c, depth, stride=8)] for c in range(4)], 0)
-        left_ref[half * LANES : (half + 1) * LANES] = stacked.T.astype(jnp.bfloat16)
+        stack_ref[half] = stacked(gather_ref, half, depth)
     matrix = matrix_ref[...]
     high = matrix.astype(jnp.bfloat16)
     wide_ref[:, :LANES] = high
     wide_ref[:, LANES:] = (matrix - high.astype(jnp.float32)).astype(jnp.bfloat16)
+
+    def one_block(block, carry):
+        gathered(gather_ref, buffers, plan.right[:sources], block)
+        for j8 in range(8):
+            for r, value in enumerate(turns(gather_ref, j8, depth)):
+                turned_ref[block, j8 * 4 + r] = value
+        return carry
+
+    if blocks == 1:
+        one_block(0, 0)
+    else:
+        lax.fori_loop(0, blocks, one_block, 0)
+
+
+def pairs_kernel(plan, *refs):
+    last_ref, wide_ref, stack_ref, turned_ref, first_ref, second_ref, out_ref = refs[:7]
+    gather_left_ref, gather_ref, left_ref, outer_ref, done_ref, sems = refs[7:]
+    first_count, second_count, _ = out_ref.shape
+    sources = len(plan.left) // 2
+    depth = sources * 2
+    width = LANES // 4
+    buffers = {plan.buffers - 1: last_ref}
+
+    gathered(gather_left_ref, buffers, plan.left[sources:], 0)
+    for half in range(2):
+        rows = jnp.concatenate([stack_ref[half], stacked(gather_left_ref, half, depth)], 0)
+        left_ref[half * LANES : (half + 1) * LANES] = rows.T.astype(jnp.bfloat16)
     first_scale = first_ref[...]
 
     def one_block(block, carry):
-        for k, (buffer, row) in enumerate(plan.right):
-            start = pl.multiple_of(row + block * ROWS, ROWS)
-            at = (sources + k) * ROWS
-            gather_ref[at : at + ROWS] = buffers[buffer][pl.ds(start, ROWS)].astype(jnp.float32)
+        gathered(gather_ref, buffers, plan.right[sources:], block)
         left = left_ref[...]
         lane_block = lax.broadcasted_iota(jnp.int32, (depth, LANES), 1) // width
         zero = jnp.zeros((depth, LANES), jnp.bfloat16)
-        turned = []
-        for j8 in range(8):
-            plain = gather_ref[pl.ds(sources * ROWS + j8, depth, stride=8)]
-            turned.append([(pltpu.roll(plain, r * width, 1) if r else plain).astype(jnp.bfloat16) for r in range(4)])
+        turned = [
+            ([turned_ref[block, j8 * 4 + r] for r in range(4)], turns(gather_ref, j8, depth)) for j8 in range(8)
+        ]
 
         def outer(q):
             for j8 in range(0, 8, 2):
                 spread = jnp.concatenate(
                     [
-                        jnp.concatenate([jnp.where(lane_block == c, t[(c - q) % 4], zero) for c in range(4)], 0)
-                        for t in turned[j8 : j8 + 2]
+                        jnp.concatenate(
+                            [jnp.where(lane_block == c, t[(c - q) % 4], zero) for t in both for c in range(4)], 0
+                        )
+                        for both in turned[j8 : j8 + 2]
                     ],
                     1,
                 )
@@ -334,22 +368,36 @@
             ways = [lambda d: masks[0]]
         buffers = buffers + [move(v, way) for v, way in zip(messages, ways)]
 
+    blocks, sources = second_count // TILE, total // 2
+    wide, stack, turned = pl.pallas_call(
+        functools.partial(ready_kernel, plan, blocks),
+        out_shape=(
+            jax.ShapeDtypeStruct((8 * LANES, 2 * LANES), bf16),
+            jax.ShapeDtypeStruct((2, 8 * sources, LANES), f32),
+            jax.ShapeDtypeStruct((blocks, 32, 2 * sources, LANES), bf16),
+        ),
+        in_specs=[vmem] * plan.buffers,
+        out_specs=(vmem,) * 3,
+        scratch_shapes=[pltpu.VMEM((sources * ROWS, LANES), f32)],
+        compiler_params=pltpu.CompilerParams(vmem_limit_bytes=VMEM_BYTES),
+        name="ready",
+    )(*buffers[:-1], matrix)
     return pl.pallas_call(
         functools.partial(pairs_kernel, plan),
         out_shape=jax.ShapeDtypeStruct((first_count, second_count, LANES), f32),
-        in_specs=[vmem] * (len(buffers) + 3),
+        in_specs=[vmem] * 6,
         out_specs=pl.BlockSpec(memory_space=pl.ANY),
         scratch_shapes=[
-            pltpu.VMEM((2 * total * ROWS, LANES), f32),
+            pltpu.VMEM((sources * ROWS, LANES), f32),
+            pltpu.VMEM((sources * ROWS, LANES), f32),
             pltpu.VMEM((2 * LANES, 4 * total * 2), bf16),
             pltpu.VMEM((first_count * TILE, 8 * LANES), bf16),
-            pltpu.VMEM((8 * LANES, 2 * LANES), bf16),
             pltpu.VMEM((4, first_count * 8, LANES), f32),
             pltpu.SemaphoreType.DMA((4,)),
         ],
         compiler_params=pltpu.CompilerParams(vmem_limit_bytes=VMEM_BYTES),
         name="pairs",
-    )(*buffers, matrix, first_scale, second_scale)
+    )(buffers[-1], wide, stack, turned, first_scale, second_scale)
 
 
 def solution(mesh):

time: 16.5 us -> 16.6 us (level)
  Pallas kernels: 3.59 us -> 3.8 us
  waiting for transfers between devices: 4.01 us -> 3.82 us
    ppermute x5, waiting for transfers between devices: 4.01 us -> 3.82 us  [per_device(): lax.ppermute(v, axes, [(d, d ^ mask_of(d)) for d in range(total)])]
    pallas_call x0 -> x1, Pallas kernels: none -> 0.19 us  [per_device(): pl.pallas_call(functools.partial(ready_kernel, plan, blocks), out_shape=(...]
  transfers between devices with their start and end apart: 5 -> 5, of which waited for: 4 -> 4; matrix products, arithmetic and copies ran while one was open for 0% -> 0% of each run, Pallas kernels for 0% -> 1%
where the time goes in v6:
time: 16.6 us; the launch traced here: 16.4 us
  starting transfers between devices  8.62 us (52%)
  waiting for transfers between devices  3.82 us (23%)
  Pallas kernels  3.8 us (23%)
    ppermute x5, starting transfers between devices, per_device(): lax.ppermute(v, axes, [(d, d ^ mask_of(d)) for d in range(total)])  8.62 us
    ppermute x5, waiting for transfers between devices, per_device(): lax.ppermute(v, axes, [(d, d ^ mask_of(d)) for d in range(total)])  3.82 us
    pallas_call x1, Pallas kernels, per_device(): pl.pallas_call(functools.partial(pairs_kernel, plan), out_shape=jax.Shape...  2.14 us
    pallas_call x1, Pallas kernels, per_device(): pl.pallas_call(functools.partial(panels_kernel, plan, split), out_shape=(...  1.48 us
  transfers between devices with their start and end apart: 5, of which 4 were waited for; matrix products, arithmetic and copies ran while one was open for 0% of the time, Pallas kernels for 1%

profile of v6, /device:TPU:0, one launch (start us, length us, event | category | flops | bytes accessed | tf_op | source)
XLA Modules:
  0.0 16.4 jit_solution(2992105451296100275)
XLA Ops:
  0.0 1.5 %panels.1 = (bf16[128,128]{1,0:T(8,128)(2,1)S(1)}, bf16[96,128]{1,0:T(8,128)(2,1)S(1)}, f32[32,128]{1,0:T(8,128)S(1)}, f32[32,128]{1,0:T(8,128)S(1)}, f32[1024,128]{1,0:T(8,128)S(1)}) custom-call(bf16[2,128,256]{2,1,0:T(8,128)(2,1)} %x_hbm.1, s32[1,128]{1,0:T(1,128)} %bitcast.11, f32[1,256]{1,0:T(1,128)} %bitcast.9, f32[1,256]{1,0:T(1,128)} %bitcast.10, ...), custom_call_target="tpu_custom_call" | custom-call | tf_op jit(solution)/shard_map/panels/pallas_call | solution.py:322
  1.5 3.5 %collective-permute-start = (bf16[96,128]{1,0:T(8,128)(2,1)S(1)}, bf16[96,128]{1,0:T(8,128)(2,1)S(1)}, u32[]{:S(2)}, u32[]{:S(2)}) collective-permute-start(bf16[96,128]{1,0:T(8,128)(2,1)S(1)} %get-tuple-element.17), channel_id=1, source_target_pairs={{0,9},{1,8},{2,11},{3,10},{4,13},{5,12},{6,15},{7,14},{8,1},{9,0},... | collective-permute-start | bytes 73736 | tf_op jit(solution)/shard_map/ppermute | solution.py:345
  5.0 1.6 %collective-permute-done.refs_1_ = bf16[96,128]{1,0:T(8,128)(2,1)S(1)} collective-permute-done((bf16[96,128]{1,0:T(8,128)(2,1)S(1)}, bf16[96,128]{1,0:T(8,128)(2,1)S(1)}, u32[]{:S(2)}, u32[]{:S(2)}) %collective-permute-start) | collective-permute-done | bytes 24608 | tf_op jit(solution)/shard_map/ppermute | solution.py:345
  6.7 1.9 %collective-permute-start.1 = (bf16[96,128]{1,0:T(8,128)(2,1)S(1)}, bf16[96,128]{1,0:T(8,128)(2,1)S(1)}, u32[]{:S(2)}, u32[]{:S(2)}) collective-permute-start(bf16[96,128]{1,0:T(8,128)(2,1)S(1)} %get-tuple-element.18), channel_id=1, source_target_pairs={{0,5},{1,4},{2,1},{3,0},{4,7},{5,6},{6,3},{7,2},{8,13},{9,12},{10,... | collective-permute-start | bytes 73736 | tf_op jit(solution)/shard_map/ppermute | solution.py:345
  8.6 0.0 collective-permute-start.2
  8.6 2.7 %collective-permute-start.3 = (bf16[96,128]{1,0:T(8,128)(2,1)S(1)}, bf16[96,128]{1,0:T(8,128)(2,1)S(1)}, u32[]{:S(2)}, u32[]{:S(2)}) collective-permute-start(bf16[96,128]{1,0:T(8,128)(2,1)S(1)} %get-tuple-element.20), channel_id=1, source_target_pairs={{0,7},{1,6},{2,5},{3,4},{4,3},{5,2},{6,1},{7,0},{8,15},{9,14},{10,... | collective-permute-start | bytes 73736 | tf_op jit(solution)/shard_map/ppermute | solution.py:345
  11.3 0.0 collective-permute-done.1.refs_2_
  11.3 0.6 %collective-permute-done.2.refs_3_ = bf16[96,128]{1,0:T(8,128)(2,1)S(1)} collective-permute-done((bf16[96,128]{1,0:T(8,128)(2,1)S(1)}, bf16[96,128]{1,0:T(8,128)(2,1)S(1)}, u32[]{:S(2)}, u32[]{:S(2)}) %collective-permute-start.2) | collective-permute-done | bytes 24608 | tf_op jit(solution)/shard_map/ppermute | solution.py:345
  11.9 0.9 %collective-permute-done.3.refs_4_ = bf16[96,128]{1,0:T(8,128)(2,1)S(1)} collective-permute-done((bf16[96,128]{1,0:T(8,128)(2,1)S(1)}, bf16[96,128]{1,0:T(8,128)(2,1)S(1)}, u32[]{:S(2)}, u32[]{:S(2)}) %collective-permute-start.3) | collective-permute-done | bytes 24608 | tf_op jit(solution)/shard_map/ppermute | solution.py:345
  12.9 0.5 %collective-permute-start.4 = (bf16[256,128]{1,0:T(8,128)(2,1)S(1)}, bf16[256,128]{1,0:T(8,128)(2,1)S(1)}, u32[]{:S(2)}, u32[]{:S(2)}) collective-permute-start(bf16[256,128]{1,0:T(8,128)(2,1)S(1)} %constant_dynamic-update-slice_fusion.18), channel_id=1, source_target_pairs={{0,1},{1,0},{2,3},{3,2},{4,5},{5,4},{6,7},{7,6},{8,9},{9,8},{10,11... | collective-permute-start | bytes 196616 | tf_op jit(solution)/shard_map/ppermute | solution.py:345
  13.4 0.2 %ready.1 = (bf16[1024,256]{1,0:T(8,128)(2,1)S(1)}, f32[2,64,128]{2,1,0:T(8,128)S(1)}, bf16[1,32,16,128]{3,2,1,0:T(8,128)(2,1)S(1)}) custom-call(bf16[128,128]{1,0:T(8,128)(2,1)S(1)} %get-tuple-element.16.refs_0_, bf16[96,128]{1,0:T(8,128)(2,1)S(1)} %collective-permute-done.refs_1_, bf16[96,128]{1,0:T(8,128)(2,1)S(1)} %collective-permute-done.1.refs_2_, ...), custom_call_target="tpu_custom_call" | custom-call | tf_op jit(solution)/shard_map/ready/pallas_call | solution.py:372
  13.6 0.7 %collective-permute-done.4.refs_0_ = bf16[256,128]{1,0:T(8,128)(2,1)S(1)} collective-permute-done((bf16[256,128]{1,0:T(8,128)(2,1)S(1)}, bf16[256,128]{1,0:T(8,128)(2,1)S(1)}, u32[]{:S(2)}, u32[]{:S(2)}) %collective-permute-start.4) | collective-permute-done | bytes 65568 | tf_op jit(solution)/shard_map/ppermute | solution.py:345
  14.3 2.1 %pairs.1 = f32[32,32,128]{2,1,0:T(8,128)} custom-call(bf16[256,128]{1,0:T(8,128)(2,1)S(1)} %collective-permute-done.4.refs_0_, bf16[1024,256]{1,0:T(8,128)(2,1)S(1)} %get-tuple-element.22.refs_1_, f32[2,64,128]{2,1,0:T(8,128)S(1)} %get-tuple-element.23.refs_2_, bf16[1,32,16,128]{3,2,1,0:T(8,128)(2,1)S(1)} %get-tuple-element.24.refs_3_, ...), custom_call_target="tpu_custom_call" | custom-call | tf_op jit(solution)/shard_map/pairs/pallas_call | solution.py:385
  (18 shorter events, 0.1 us)
Async XLA Ops:
  1.5 5.1 %collective-permute-start = (bf16[96,128]{1,0:T(8,128)(2,1)S(1)}, bf16[96,128]{1,0:T(8,128)(2,1)S(1)}, u32[]{:S(2)}, u32[]{:S(2)}) collective-permute-start(bf16[96,128]{1,0:T(8,128)(2,1)S(1)} %get-tuple-element.17), channel_id=1, source_target_pairs={{0,9},{1,8},{2,11},{3,10},{4,13},{5,12},{6,15},{7,14},{8,1},{9,0},... | collective-permute-start | bytes 73736 | tf_op jit(solution)/shard_map/ppermute | solution.py:345
  6.7 4.6 %collective-permute-start.1 = (bf16[96,128]{1,0:T(8,128)(2,1)S(1)}, bf16[96,128]{1,0:T(8,128)(2,1)S(1)}, u32[]{:S(2)}, u32[]{:S(2)}) collective-permute-start(bf16[96,128]{1,0:T(8,128)(2,1)S(1)} %get-tuple-element.18), channel_id=1, source_target_pairs={{0,5},{1,4},{2,1},{3,0},{4,7},{5,6},{6,3},{7,2},{8,13},{9,12},{10,... | collective-permute-start | bytes 73736 | tf_op jit(solution)/shard_map/ppermute | solution.py:345
  8.6 3.3 %collective-permute-start.2 = (bf16[96,128]{1,0:T(8,128)(2,1)S(1)}, bf16[96,128]{1,0:T(8,128)(2,1)S(1)}, u32[]{:S(2)}, u32[]{:S(2)}) collective-permute-start(bf16[96,128]{1,0:T(8,128)(2,1)S(1)} %get-tuple-element.19), channel_id=1, source_target_pairs={{0,3},{1,2},{2,7},{3,6},{4,1},{5,0},{6,5},{7,4},{8,11},{9,10},{10,... | collective-permute-start | bytes 73736 | tf_op jit(solution)/shard_map/ppermute | solution.py:345
  8.6 4.2 %collective-permute-start.3 = (bf16[96,128]{1,0:T(8,128)(2,1)S(1)}, bf16[96,128]{1,0:T(8,128)(2,1)S(1)}, u32[]{:S(2)}, u32[]{:S(2)}) collective-permute-start(bf16[96,128]{1,0:T(8,128)(2,1)S(1)} %get-tuple-element.20), channel_id=1, source_target_pairs={{0,7},{1,6},{2,5},{3,4},{4,3},{5,2},{6,1},{7,0},{8,15},{9,14},{10,... | collective-permute-start | bytes 73736 | tf_op jit(solution)/shard_map/ppermute | solution.py:345
  12.9 1.4 %collective-permute-start.4 = (bf16[256,128]{1,0:T(8,128)(2,1)S(1)}, bf16[256,128]{1,0:T(8,128)(2,1)S(1)}, u32[]{:S(2)}, u32[]{:S(2)}) collective-permute-start(bf16[256,128]{1,0:T(8,128)(2,1)S(1)} %constant_dynamic-update-slice_fusion.18), channel_id=1, source_target_pairs={{0,1},{1,0},{2,3},{3,2},{4,5},{5,4},{6,7},{7,6},{8,9},{9,8},{10,11... | collective-permute-start | bytes 196616 | tf_op jit(solution)/shard_map/ppermute | solution.py:345

commit v7 on v6

--- a/solution.py
+++ b/solution.py
@@ -355,15 +355,15 @@
             ]
         if len(masks) == 3:
             one, two, across = masks
-            low, high = one & ~core, two & ~core
-            even = lambda d: ((d & low) != 0) == ((d & high) != 0)
+            high = two & ~core
+            odd = lambda d: (d & high) != 0
             messages = [
-                jnp.where(even(me), messages[1], messages[0]),
-                jnp.where(even(me), messages[0], messages[1]),
-                messages[2],
+                jnp.where(odd(me), messages[2], messages[1]),
+                jnp.where(odd(me), messages[1], messages[2]),
+                messages[0],
             ]
             messages = list(lax.optimization_barrier(tuple(messages)))
-            ways = [lambda d: two if even(d) else one, lambda d: one if even(d) else two, lambda d: across]
+            ways = [lambda d: across if odd(d) else two, lambda d: two if odd(d) else across, lambda d: one]
         else:
             ways = [lambda d: masks[0]]
         buffers = buffers + [move(v, way) for v, way in zip(messages, ways)]

time: 16.6 us -> 16.6 us (level)
  no operation moved by 1% of the time
where the time goes in v7:
time: 16.6 us; the launch traced here: 16.4 us
  starting transfers between devices  8.48 us (51%)
  waiting for transfers between devices  3.98 us (24%)
  Pallas kernels  3.79 us (23%)
    ppermute x5, starting transfers between devices, per_device(): lax.ppermute(v, axes, [(d, d ^ mask_of(d)) for d in range(total)])  8.48 us
    ppermute x5, waiting for transfers between devices, per_device(): lax.ppermute(v, axes, [(d, d ^ mask_of(d)) for d in range(total)])  3.98 us
    pallas_call x1, Pallas kernels, per_device(): pl.pallas_call(functools.partial(pairs_kernel, plan), out_shape=jax.Shape...  2.12 us
    pallas_call x1, Pallas kernels, per_device(): pl.pallas_call(functools.partial(panels_kernel, plan, split), out_shape=(...  1.48 us
  transfers between devices with their start and end apart: 5, of which 4 were waited for; matrix products, arithmetic and copies ran while one was open for 0% of the time, Pallas kernels for 1%

profile of v7, /device:TPU:0, one launch (start us, length us, event | category | flops | bytes accessed | tf_op | source)
XLA Modules:
  0.0 16.4 jit_solution(14149496371097331492)
XLA Ops:
  0.0 1.5 %panels.1 = (bf16[128,128]{1,0:T(8,128)(2,1)S(1)}, bf16[96,128]{1,0:T(8,128)(2,1)S(1)}, f32[32,128]{1,0:T(8,128)S(1)}, f32[32,128]{1,0:T(8,128)S(1)}, f32[1024,128]{1,0:T(8,128)S(1)}) custom-call(bf16[2,128,256]{2,1,0:T(8,128)(2,1)} %x_hbm.1, s32[1,128]{1,0:T(1,128)} %bitcast.11, f32[1,256]{1,0:T(1,128)} %bitcast.9, f32[1,256]{1,0:T(1,128)} %bitcast.10, ...), custom_call_target="tpu_custom_call" | custom-call | tf_op jit(solution)/shard_map/panels/pallas_call | solution.py:322
  1.5 3.5 %collective-permute-start = (bf16[96,128]{1,0:T(8,128)(2,1)S(1)}, bf16[96,128]{1,0:T(8,128)(2,1)S(1)}, u32[]{:S(2)}, u32[]{:S(2)}) collective-permute-start(bf16[96,128]{1,0:T(8,128)(2,1)S(1)} %get-tuple-element.17), channel_id=1, source_target_pairs={{0,9},{1,8},{2,11},{3,10},{4,13},{5,12},{6,15},{7,14},{8,1},{9,0},... | collective-permute-start | bytes 73736 | tf_op jit(solution)/shard_map/ppermute | solution.py:345
  5.0 1.6 %collective-permute-done.refs_1_ = bf16[96,128]{1,0:T(8,128)(2,1)S(1)} collective-permute-done((bf16[96,128]{1,0:T(8,128)(2,1)S(1)}, bf16[96,128]{1,0:T(8,128)(2,1)S(1)}, u32[]{:S(2)}, u32[]{:S(2)}) %collective-permute-start) | collective-permute-done | bytes 24608 | tf_op jit(solution)/shard_map/ppermute | solution.py:345
  6.7 1.9 %collective-permute-start.1 = (bf16[96,128]{1,0:T(8,128)(2,1)S(1)}, bf16[96,128]{1,0:T(8,128)(2,1)S(1)}, u32[]{:S(2)}, u32[]{:S(2)}) collective-permute-start(bf16[96,128]{1,0:T(8,128)(2,1)S(1)} %get-tuple-element.18), channel_id=1, source_target_pairs={{0,5},{1,4},{2,7},{3,6},{4,3},{5,2},{6,1},{7,0},{8,13},{9,12},{10,... | collective-permute-start | bytes 73736 | tf_op jit(solution)/shard_map/ppermute | solution.py:345
  8.6 1.0 %collective-permute-start.2 = (bf16[96,128]{1,0:T(8,128)(2,1)S(1)}, bf16[96,128]{1,0:T(8,128)(2,1)S(1)}, u32[]{:S(2)}, u32[]{:S(2)}) collective-permute-start(bf16[96,128]{1,0:T(8,128)(2,1)S(1)} %get-tuple-element.19), channel_id=1, source_target_pairs={{0,7},{1,6},{2,5},{3,4},{4,1},{5,0},{6,3},{7,2},{8,15},{9,14},{10,... | collective-permute-start | bytes 73736 | tf_op jit(solution)/shard_map/ppermute | solution.py:345
  9.6 1.6 %collective-permute-start.3 = (bf16[96,128]{1,0:T(8,128)(2,1)S(1)}, bf16[96,128]{1,0:T(8,128)(2,1)S(1)}, u32[]{:S(2)}, u32[]{:S(2)}) collective-permute-start(bf16[96,128]{1,0:T(8,128)(2,1)S(1)} %get-tuple-element.20), channel_id=1, source_target_pairs={{0,3},{1,2},{2,1},{3,0},{4,7},{5,6},{6,5},{7,4},{8,11},{9,10},{10,... | collective-permute-start | bytes 73736 | tf_op jit(solution)/shard_map/ppermute | solution.py:345
  11.2 0.0 collective-permute-done.1.refs_2_
  11.2 0.9 %collective-permute-done.2.refs_3_ = bf16[96,128]{1,0:T(8,128)(2,1)S(1)} collective-permute-done((bf16[96,128]{1,0:T(8,128)(2,1)S(1)}, bf16[96,128]{1,0:T(8,128)(2,1)S(1)}, u32[]{:S(2)}, u32[]{:S(2)}) %collective-permute-start.2) | collective-permute-done | bytes 24608 | tf_op jit(solution)/shard_map/ppermute | solution.py:345
  12.1 0.8 %collective-permute-done.3.refs_4_ = bf16[96,128]{1,0:T(8,128)(2,1)S(1)} collective-permute-done((bf16[96,128]{1,0:T(8,128)(2,1)S(1)}, bf16[96,128]{1,0:T(8,128)(2,1)S(1)}, u32[]{:S(2)}, u32[]{:S(2)}) %collective-permute-start.3) | collective-permute-done | bytes 24608 | tf_op jit(solution)/shard_map/ppermute | solution.py:345
  12.9 0.5 %collective-permute-start.4 = (bf16[256,128]{1,0:T(8,128)(2,1)S(1)}, bf16[256,128]{1,0:T(8,128)(2,1)S(1)}, u32[]{:S(2)}, u32[]{:S(2)}) collective-permute-start(bf16[256,128]{1,0:T(8,128)(2,1)S(1)} %constant_dynamic-update-slice_fusion.18), channel_id=1, source_target_pairs={{0,1},{1,0},{2,3},{3,2},{4,5},{5,4},{6,7},{7,6},{8,9},{9,8},{10,11... | collective-permute-start | bytes 196616 | tf_op jit(solution)/shard_map/ppermute | solution.py:345
  13.4 0.2 %ready.1 = (bf16[1024,256]{1,0:T(8,128)(2,1)S(1)}, f32[2,64,128]{2,1,0:T(8,128)S(1)}, bf16[1,32,16,128]{3,2,1,0:T(8,128)(2,1)S(1)}) custom-call(bf16[128,128]{1,0:T(8,128)(2,1)S(1)} %get-tuple-element.16.refs_0_, bf16[96,128]{1,0:T(8,128)(2,1)S(1)} %collective-permute-done.refs_1_, bf16[96,128]{1,0:T(8,128)(2,1)S(1)} %collective-permute-done.1.refs_2_, ...), custom_call_target="tpu_custom_call" | custom-call | tf_op jit(solution)/shard_map/ready/pallas_call | solution.py:372
  13.6 0.7 %collective-permute-done.4.refs_0_ = bf16[256,128]{1,0:T(8,128)(2,1)S(1)} collective-permute-done((bf16[256,128]{1,0:T(8,128)(2,1)S(1)}, bf16[256,128]{1,0:T(8,128)(2,1)S(1)}, u32[]{:S(2)}, u32[]{:S(2)}) %collective-permute-start.4) | collective-permute-done | bytes 65568 | tf_op jit(solution)/shard_map/ppermute | solution.py:345
  14.3 2.1 %pairs.1 = f32[32,32,128]{2,1,0:T(8,128)} custom-call(bf16[256,128]{1,0:T(8,128)(2,1)S(1)} %collective-permute-done.4.refs_0_, bf16[1024,256]{1,0:T(8,128)(2,1)S(1)} %get-tuple-element.22.refs_1_, f32[2,64,128]{2,1,0:T(8,128)S(1)} %get-tuple-element.23.refs_2_, bf16[1,32,16,128]{3,2,1,0:T(8,128)(2,1)S(1)} %get-tuple-element.24.refs_3_, ...), custom_call_target="tpu_custom_call" | custom-call | tf_op jit(solution)/shard_map/pairs/pallas_call | solution.py:385
  (18 shorter events, 0.1 us)
Async XLA Ops:
  1.5 5.1 %collective-permute-start = (bf16[96,128]{1,0:T(8,128)(2,1)S(1)}, bf16[96,128]{1,0:T(8,128)(2,1)S(1)}, u32[]{:S(2)}, u32[]{:S(2)}) collective-permute-start(bf16[96,128]{1,0:T(8,128)(2,1)S(1)} %get-tuple-element.17), channel_id=1, source_target_pairs={{0,9},{1,8},{2,11},{3,10},{4,13},{5,12},{6,15},{7,14},{8,1},{9,0},... | collective-permute-start | bytes 73736 | tf_op jit(solution)/shard_map/ppermute | solution.py:345
  6.7 4.4 %collective-permute-start.1 = (bf16[96,128]{1,0:T(8,128)(2,1)S(1)}, bf16[96,128]{1,0:T(8,128)(2,1)S(1)}, u32[]{:S(2)}, u32[]{:S(2)}) collective-permute-start(bf16[96,128]{1,0:T(8,128)(2,1)S(1)} %get-tuple-element.18), channel_id=1, source_target_pairs={{0,5},{1,4},{2,7},{3,6},{4,3},{5,2},{6,1},{7,0},{8,13},{9,12},{10,... | collective-permute-start | bytes 73736 | tf_op jit(solution)/shard_map/ppermute | solution.py:345
  8.6 3.4 %collective-permute-start.2 = (bf16[96,128]{1,0:T(8,128)(2,1)S(1)}, bf16[96,128]{1,0:T(8,128)(2,1)S(1)}, u32[]{:S(2)}, u32[]{:S(2)}) collective-permute-start(bf16[96,128]{1,0:T(8,128)(2,1)S(1)} %get-tuple-element.19), channel_id=1, source_target_pairs={{0,7},{1,6},{2,5},{3,4},{4,1},{5,0},{6,3},{7,2},{8,15},{9,14},{10,... | collective-permute-start | bytes 73736 | tf_op jit(solution)/shard_map/ppermute | solution.py:345
  9.6 3.3 %collective-permute-start.3 = (bf16[96,128]{1,0:T(8,128)(2,1)S(1)}, bf16[96,128]{1,0:T(8,128)(2,1)S(1)}, u32[]{:S(2)}, u32[]{:S(2)}) collective-permute-start(bf16[96,128]{1,0:T(8,128)(2,1)S(1)} %get-tuple-element.20), channel_id=1, source_target_pairs={{0,3},{1,2},{2,1},{3,0},{4,7},{5,6},{6,5},{7,4},{8,11},{9,10},{10,... | collective-permute-start | bytes 73736 | tf_op jit(solution)/shard_map/ppermute | solution.py:345
  12.9 1.4 %collective-permute-start.4 = (bf16[256,128]{1,0:T(8,128)(2,1)S(1)}, bf16[256,128]{1,0:T(8,128)(2,1)S(1)}, u32[]{:S(2)}, u32[]{:S(2)}) collective-permute-start(bf16[256,128]{1,0:T(8,128)(2,1)S(1)} %constant_dynamic-update-slice_fusion.18), channel_id=1, source_target_pairs={{0,1},{1,0},{2,3},{3,2},{4,5},{5,4},{6,7},{7,6},{8,9},{9,8},{10,11... | collective-permute-start | bytes 196616 | tf_op jit(solution)/shard_map/ppermute | solution.py:345

commit v8 on v6

--- a/solution.py
+++ b/solution.py
@@ -85,8 +85,12 @@
     for copy in copies_in:
         copy.start()
     matrix_copy.start()
-    for copy in copies_in:
+    x_copy, *others = copies_in
+    for copy in others:
         copy.wait()
+    copies = LANES // width
+    matrix = jnp.concatenate([latter_ref[...]] * copies + [former_ref[...]] * copies, axis=0).T
+    x_copy.wait()
 
     x = x_ref[...].reshape(depth * chain, features).astype(jnp.float32)
     center = x - jnp.mean(x, axis=-1, keepdims=True)
@@ -95,11 +99,8 @@
     normed = normed.astype(jnp.bfloat16)
 
     copies = LANES // width
-    latter = latter_ref[...]
-    former = former_ref[...]
-    matrix = jnp.concatenate([latter] * copies + [former] * copies, axis=0)
     bias = jnp.concatenate([latter_bias_ref[...]] * copies + [former_bias_ref[...]] * copies, axis=1)
-    both = lax.dot_general(normed, matrix, (((1,), (1,)), ((), ())), preferred_element_type=jnp.float32) + bias
+    both = lax.dot_general(normed, matrix, (((1,), (0,)), ((), ())), preferred_element_type=jnp.float32) + bias
 
     tallies = tallies_ref[...]
     lane_block = lax.broadcasted_iota(jnp.int32, (8, LANES), 1) // TILE

time: 16.6 us -> 16.6 us (level)
  no operation moved by 1% of the time
where the time goes in v8:
time: 16.6 us; the launch traced here: 16.4 us
  starting transfers between devices  8.62 us (52%)
  waiting for transfers between devices  3.82 us (23%)
  Pallas kernels  3.79 us (23%)
    ppermute x5, starting transfers between devices, per_device(): lax.ppermute(v, axes, [(d, d ^ mask_of(d)) for d in range(total)])  8.62 us
    ppermute x5, waiting for transfers between devices, per_device(): lax.ppermute(v, axes, [(d, d ^ mask_of(d)) for d in range(total)])  3.82 us
    pallas_call x1, Pallas kernels, per_device(): pl.pallas_call(functools.partial(pairs_kernel, plan), out_shape=jax.Shape...  2.14 us
    pallas_call x1, Pallas kernels, per_device(): pl.pallas_call(functools.partial(panels_kernel, plan, split), out_shape=(...  1.47 us
  transfers between devices with their start and end apart: 5, of which 4 were waited for; matrix products, arithmetic and copies ran while one was open for 0% of the time, Pallas kernels for 1%

profile of v8, /device:TPU:0, one launch (start us, length us, event | category | flops | bytes accessed | tf_op | source)
XLA Modules:
  0.0 16.4 jit_solution(9786171880940263205)
XLA Ops:
  0.0 1.5 %panels.1 = (bf16[128,128]{1,0:T(8,128)(2,1)S(1)}, bf16[96,128]{1,0:T(8,128)(2,1)S(1)}, f32[32,128]{1,0:T(8,128)S(1)}, f32[32,128]{1,0:T(8,128)S(1)}, f32[1024,128]{1,0:T(8,128)S(1)}) custom-call(bf16[2,128,256]{2,1,0:T(8,128)(2,1)} %x_hbm.1, s32[1,128]{1,0:T(1,128)} %bitcast.11, f32[1,256]{1,0:T(1,128)} %bitcast.9, f32[1,256]{1,0:T(1,128)} %bitcast.10, ...), custom_call_target="tpu_custom_call" | custom-call | tf_op jit(solution)/shard_map/panels/pallas_call | solution.py:323
  1.5 3.5 %collective-permute-start = (bf16[96,128]{1,0:T(8,128)(2,1)S(1)}, bf16[96,128]{1,0:T(8,128)(2,1)S(1)}, u32[]{:S(2)}, u32[]{:S(2)}) collective-permute-start(bf16[96,128]{1,0:T(8,128)(2,1)S(1)} %get-tuple-element.17), channel_id=1, source_target_pairs={{0,9},{1,8},{2,11},{3,10},{4,13},{5,12},{6,15},{7,14},{8,1},{9,0},... | collective-permute-start | bytes 73736 | tf_op jit(solution)/shard_map/ppermute | solution.py:346
  5.0 1.6 %collective-permute-done.refs_1_ = bf16[96,128]{1,0:T(8,128)(2,1)S(1)} collective-permute-done((bf16[96,128]{1,0:T(8,128)(2,1)S(1)}, bf16[96,128]{1,0:T(8,128)(2,1)S(1)}, u32[]{:S(2)}, u32[]{:S(2)}) %collective-permute-start) | collective-permute-done | bytes 24608 | tf_op jit(solution)/shard_map/ppermute | solution.py:346
  6.7 1.9 %collective-permute-start.1 = (bf16[96,128]{1,0:T(8,128)(2,1)S(1)}, bf16[96,128]{1,0:T(8,128)(2,1)S(1)}, u32[]{:S(2)}, u32[]{:S(2)}) collective-permute-start(bf16[96,128]{1,0:T(8,128)(2,1)S(1)} %get-tuple-element.18), channel_id=1, source_target_pairs={{0,5},{1,4},{2,1},{3,0},{4,7},{5,6},{6,3},{7,2},{8,13},{9,12},{10,... | collective-permute-start | bytes 73736 | tf_op jit(solution)/shard_map/ppermute | solution.py:346
  8.6 0.0 collective-permute-start.2
  8.6 2.7 %collective-permute-start.3 = (bf16[96,128]{1,0:T(8,128)(2,1)S(1)}, bf16[96,128]{1,0:T(8,128)(2,1)S(1)}, u32[]{:S(2)}, u32[]{:S(2)}) collective-permute-start(bf16[96,128]{1,0:T(8,128)(2,1)S(1)} %get-tuple-element.20), channel_id=1, source_target_pairs={{0,7},{1,6},{2,5},{3,4},{4,3},{5,2},{6,1},{7,0},{8,15},{9,14},{10,... | collective-permute-start | bytes 73736 | tf_op jit(solution)/shard_map/ppermute | solution.py:346
  11.3 0.0 collective-permute-done.1.refs_2_
  11.3 0.6 %collective-permute-done.2.refs_3_ = bf16[96,128]{1,0:T(8,128)(2,1)S(1)} collective-permute-done((bf16[96,128]{1,0:T(8,128)(2,1)S(1)}, bf16[96,128]{1,0:T(8,128)(2,1)S(1)}, u32[]{:S(2)}, u32[]{:S(2)}) %collective-permute-start.2) | collective-permute-done | bytes 24608 | tf_op jit(solution)/shard_map/ppermute | solution.py:346
  11.9 0.9 %collective-permute-done.3.refs_4_ = bf16[96,128]{1,0:T(8,128)(2,1)S(1)} collective-permute-done((bf16[96,128]{1,0:T(8,128)(2,1)S(1)}, bf16[96,128]{1,0:T(8,128)(2,1)S(1)}, u32[]{:S(2)}, u32[]{:S(2)}) %collective-permute-start.3) | collective-permute-done | bytes 24608 | tf_op jit(solution)/shard_map/ppermute | solution.py:346
  12.8 0.5 %collective-permute-start.4 = (bf16[256,128]{1,0:T(8,128)(2,1)S(1)}, bf16[256,128]{1,0:T(8,128)(2,1)S(1)}, u32[]{:S(2)}, u32[]{:S(2)}) collective-permute-start(bf16[256,128]{1,0:T(8,128)(2,1)S(1)} %constant_dynamic-update-slice_fusion.18), channel_id=1, source_target_pairs={{0,1},{1,0},{2,3},{3,2},{4,5},{5,4},{6,7},{7,6},{8,9},{9,8},{10,11... | collective-permute-start | bytes 196616 | tf_op jit(solution)/shard_map/ppermute | solution.py:346
  13.4 0.2 %ready.1 = (bf16[1024,256]{1,0:T(8,128)(2,1)S(1)}, f32[2,64,128]{2,1,0:T(8,128)S(1)}, bf16[1,32,16,128]{3,2,1,0:T(8,128)(2,1)S(1)}) custom-call(bf16[128,128]{1,0:T(8,128)(2,1)S(1)} %get-tuple-element.16.refs_0_, bf16[96,128]{1,0:T(8,128)(2,1)S(1)} %collective-permute-done.refs_1_, bf16[96,128]{1,0:T(8,128)(2,1)S(1)} %collective-permute-done.1.refs_2_, ...), custom_call_target="tpu_custom_call" | custom-call | tf_op jit(solution)/shard_map/ready/pallas_call | solution.py:373
  13.6 0.7 %collective-permute-done.4.refs_0_ = bf16[256,128]{1,0:T(8,128)(2,1)S(1)} collective-permute-done((bf16[256,128]{1,0:T(8,128)(2,1)S(1)}, bf16[256,128]{1,0:T(8,128)(2,1)S(1)}, u32[]{:S(2)}, u32[]{:S(2)}) %collective-permute-start.4) | collective-permute-done | bytes 65568 | tf_op jit(solution)/shard_map/ppermute | solution.py:346
  14.3 2.1 %pairs.1 = f32[32,32,128]{2,1,0:T(8,128)} custom-call(bf16[256,128]{1,0:T(8,128)(2,1)S(1)} %collective-permute-done.4.refs_0_, bf16[1024,256]{1,0:T(8,128)(2,1)S(1)} %get-tuple-element.22.refs_1_, f32[2,64,128]{2,1,0:T(8,128)S(1)} %get-tuple-element.23.refs_2_, bf16[1,32,16,128]{3,2,1,0:T(8,128)(2,1)S(1)} %get-tuple-element.24.refs_3_, ...), custom_call_target="tpu_custom_call" | custom-call | tf_op jit(solution)/shard_map/pairs/pallas_call | solution.py:386
  (18 shorter events, 0.1 us)
Async XLA Ops:
  1.5 5.2 %collective-permute-start = (bf16[96,128]{1,0:T(8,128)(2,1)S(1)}, bf16[96,128]{1,0:T(8,128)(2,1)S(1)}, u32[]{:S(2)}, u32[]{:S(2)}) collective-permute-start(bf16[96,128]{1,0:T(8,128)(2,1)S(1)} %get-tuple-element.17), channel_id=1, source_target_pairs={{0,9},{1,8},{2,11},{3,10},{4,13},{5,12},{6,15},{7,14},{8,1},{9,0},... | collective-permute-start | bytes 73736 | tf_op jit(solution)/shard_map/ppermute | solution.py:346
  6.7 4.6 %collective-permute-start.1 = (bf16[96,128]{1,0:T(8,128)(2,1)S(1)}, bf16[96,128]{1,0:T(8,128)(2,1)S(1)}, u32[]{:S(2)}, u32[]{:S(2)}) collective-permute-start(bf16[96,128]{1,0:T(8,128)(2,1)S(1)} %get-tuple-element.18), channel_id=1, source_target_pairs={{0,5},{1,4},{2,1},{3,0},{4,7},{5,6},{6,3},{7,2},{8,13},{9,12},{10,... | collective-permute-start | bytes 73736 | tf_op jit(solution)/shard_map/ppermute | solution.py:346
  8.6 3.3 %collective-permute-start.2 = (bf16[96,128]{1,0:T(8,128)(2,1)S(1)}, bf16[96,128]{1,0:T(8,128)(2,1)S(1)}, u32[]{:S(2)}, u32[]{:S(2)}) collective-permute-start(bf16[96,128]{1,0:T(8,128)(2,1)S(1)} %get-tuple-element.19), channel_id=1, source_target_pairs={{0,3},{1,2},{2,7},{3,6},{4,1},{5,0},{6,5},{7,4},{8,11},{9,10},{10,... | collective-permute-start | bytes 73736 | tf_op jit(solution)/shard_map/ppermute | solution.py:346
  8.6 4.2 %collective-permute-start.3 = (bf16[96,128]{1,0:T(8,128)(2,1)S(1)}, bf16[96,128]{1,0:T(8,128)(2,1)S(1)}, u32[]{:S(2)}, u32[]{:S(2)}) collective-permute-start(bf16[96,128]{1,0:T(8,128)(2,1)S(1)} %get-tuple-element.20), channel_id=1, source_target_pairs={{0,7},{1,6},{2,5},{3,4},{4,3},{5,2},{6,1},{7,0},{8,15},{9,14},{10,... | collective-permute-start | bytes 73736 | tf_op jit(solution)/shard_map/ppermute | solution.py:346
  12.8 1.4 %collective-permute-start.4 = (bf16[256,128]{1,0:T(8,128)(2,1)S(1)}, bf16[256,128]{1,0:T(8,128)(2,1)S(1)}, u32[]{:S(2)}, u32[]{:S(2)}) collective-permute-start(bf16[256,128]{1,0:T(8,128)(2,1)S(1)} %constant_dynamic-update-slice_fusion.18), channel_id=1, source_target_pairs={{0,1},{1,0},{2,3},{3,2},{4,5},{5,4},{6,7},{7,6},{8,9},{9,8},{10,11... | collective-permute-start | bytes 196616 | tf_op jit(solution)/shard_map/ppermute | solution.py:346

commit v9 on v6

--- a/solution.py
+++ b/solution.py
@@ -255,11 +255,10 @@
             )
 
         outer(0)
-        outer(1)
         copies = []
         for q in range(4):
-            if q + 2 < 4:
-                outer(q + 2)
+            if q + 1 < 4:
+                outer(q + 1)
             copies.append(project(q))
             copies[-1].start()
         for copy in copies:

time: 16.6 us -> 16.6 us (level)
  no operation moved by 1% of the time
where the time goes in v9:
time: 16.6 us; the launch traced here: 16.4 us
  starting transfers between devices  8.62 us (52%)
  waiting for transfers between devices  3.82 us (23%)
  Pallas kernels  3.81 us (23%)
    ppermute x5, starting transfers between devices, per_device(): lax.ppermute(v, axes, [(d, d ^ mask_of(d)) for d in range(total)])  8.62 us
    ppermute x5, waiting for transfers between devices, per_device(): lax.ppermute(v, axes, [(d, d ^ mask_of(d)) for d in range(total)])  3.82 us
    pallas_call x1, Pallas kernels, per_device(): pl.pallas_call(functools.partial(pairs_kernel, plan), out_shape=jax.Shape...  2.14 us
    pallas_call x1, Pallas kernels, per_device(): pl.pallas_call(functools.partial(panels_kernel, plan, split), out_shape=(...  1.48 us
  transfers between devices with their start and end apart: 5, of which 4 were waited for; matrix products, arithmetic and copies ran while one was open for 0% of the time, Pallas kernels for 1%

profile of v9, /device:TPU:0, one launch (start us, length us, event | category | flops | bytes accessed | tf_op | source)
XLA Modules:
  0.0 16.4 jit_solution(2277458960537302725)
XLA Ops:
  0.0 1.5 %panels.1 = (bf16[128,128]{1,0:T(8,128)(2,1)S(1)}, bf16[96,128]{1,0:T(8,128)(2,1)S(1)}, f32[32,128]{1,0:T(8,128)S(1)}, f32[32,128]{1,0:T(8,128)S(1)}, f32[1024,128]{1,0:T(8,128)S(1)}) custom-call(bf16[2,128,256]{2,1,0:T(8,128)(2,1)} %x_hbm.1, s32[1,128]{1,0:T(1,128)} %bitcast.11, f32[1,256]{1,0:T(1,128)} %bitcast.9, f32[1,256]{1,0:T(1,128)} %bitcast.10, ...), custom_call_target="tpu_custom_call" | custom-call | tf_op jit(solution)/shard_map/panels/pallas_call | solution.py:321
  1.5 3.5 %collective-permute-start = (bf16[96,128]{1,0:T(8,128)(2,1)S(1)}, bf16[96,128]{1,0:T(8,128)(2,1)S(1)}, u32[]{:S(2)}, u32[]{:S(2)}) collective-permute-start(bf16[96,128]{1,0:T(8,128)(2,1)S(1)} %get-tuple-element.17), channel_id=1, source_target_pairs={{0,9},{1,8},{2,11},{3,10},{4,13},{5,12},{6,15},{7,14},{8,1},{9,0},... | collective-permute-start | bytes 73736 | tf_op jit(solution)/shard_map/ppermute | solution.py:344
  5.0 1.6 %collective-permute-done.refs_1_ = bf16[96,128]{1,0:T(8,128)(2,1)S(1)} collective-permute-done((bf16[96,128]{1,0:T(8,128)(2,1)S(1)}, bf16[96,128]{1,0:T(8,128)(2,1)S(1)}, u32[]{:S(2)}, u32[]{:S(2)}) %collective-permute-start) | collective-permute-done | bytes 24608 | tf_op jit(solution)/shard_map/ppermute | solution.py:344
  6.7 1.9 %collective-permute-start.1 = (bf16[96,128]{1,0:T(8,128)(2,1)S(1)}, bf16[96,128]{1,0:T(8,128)(2,1)S(1)}, u32[]{:S(2)}, u32[]{:S(2)}) collective-permute-start(bf16[96,128]{1,0:T(8,128)(2,1)S(1)} %get-tuple-element.18), channel_id=1, source_target_pairs={{0,5},{1,4},{2,1},{3,0},{4,7},{5,6},{6,3},{7,2},{8,13},{9,12},{10,... | collective-permute-start | bytes 73736 | tf_op jit(solution)/shard_map/ppermute | solution.py:344
  8.6 0.0 collective-permute-start.2
  8.6 2.7 %collective-permute-start.3 = (bf16[96,128]{1,0:T(8,128)(2,1)S(1)}, bf16[96,128]{1,0:T(8,128)(2,1)S(1)}, u32[]{:S(2)}, u32[]{:S(2)}) collective-permute-start(bf16[96,128]{1,0:T(8,128)(2,1)S(1)} %get-tuple-element.20), channel_id=1, source_target_pairs={{0,7},{1,6},{2,5},{3,4},{4,3},{5,2},{6,1},{7,0},{8,15},{9,14},{10,... | collective-permute-start | bytes 73736 | tf_op jit(solution)/shard_map/ppermute | solution.py:344
  11.3 0.0 collective-permute-done.1.refs_2_
  11.3 0.6 %collective-permute-done.2.refs_3_ = bf16[96,128]{1,0:T(8,128)(2,1)S(1)} collective-permute-done((bf16[96,128]{1,0:T(8,128)(2,1)S(1)}, bf16[96,128]{1,0:T(8,128)(2,1)S(1)}, u32[]{:S(2)}, u32[]{:S(2)}) %collective-permute-start.2) | collective-permute-done | bytes 24608 | tf_op jit(solution)/shard_map/ppermute | solution.py:344
  11.9 0.9 %collective-permute-done.3.refs_4_ = bf16[96,128]{1,0:T(8,128)(2,1)S(1)} collective-permute-done((bf16[96,128]{1,0:T(8,128)(2,1)S(1)}, bf16[96,128]{1,0:T(8,128)(2,1)S(1)}, u32[]{:S(2)}, u32[]{:S(2)}) %collective-permute-start.3) | collective-permute-done | bytes 24608 | tf_op jit(solution)/shard_map/ppermute | solution.py:344
  12.9 0.5 %collective-permute-start.4 = (bf16[256,128]{1,0:T(8,128)(2,1)S(1)}, bf16[256,128]{1,0:T(8,128)(2,1)S(1)}, u32[]{:S(2)}, u32[]{:S(2)}) collective-permute-start(bf16[256,128]{1,0:T(8,128)(2,1)S(1)} %constant_dynamic-update-slice_fusion.18), channel_id=1, source_target_pairs={{0,1},{1,0},{2,3},{3,2},{4,5},{5,4},{6,7},{7,6},{8,9},{9,8},{10,11... | collective-permute-start | bytes 196616 | tf_op jit(solution)/shard_map/ppermute | solution.py:344
  13.4 0.2 %ready.1 = (bf16[1024,256]{1,0:T(8,128)(2,1)S(1)}, f32[2,64,128]{2,1,0:T(8,128)S(1)}, bf16[1,32,16,128]{3,2,1,0:T(8,128)(2,1)S(1)}) custom-call(bf16[128,128]{1,0:T(8,128)(2,1)S(1)} %get-tuple-element.16.refs_0_, bf16[96,128]{1,0:T(8,128)(2,1)S(1)} %collective-permute-done.refs_1_, bf16[96,128]{1,0:T(8,128)(2,1)S(1)} %collective-permute-done.1.refs_2_, ...), custom_call_target="tpu_custom_call" | custom-call | tf_op jit(solution)/shard_map/ready/pallas_call | solution.py:371
  13.6 0.7 %collective-permute-done.4.refs_0_ = bf16[256,128]{1,0:T(8,128)(2,1)S(1)} collective-permute-done((bf16[256,128]{1,0:T(8,128)(2,1)S(1)}, bf16[256,128]{1,0:T(8,128)(2,1)S(1)}, u32[]{:S(2)}, u32[]{:S(2)}) %collective-permute-start.4) | collective-permute-done | bytes 65568 | tf_op jit(solution)/shard_map/ppermute | solution.py:344
  14.3 2.1 %pairs.1 = f32[32,32,128]{2,1,0:T(8,128)} custom-call(bf16[256,128]{1,0:T(8,128)(2,1)S(1)} %collective-permute-done.4.refs_0_, bf16[1024,256]{1,0:T(8,128)(2,1)S(1)} %get-tuple-element.22.refs_1_, f32[2,64,128]{2,1,0:T(8,128)S(1)} %get-tuple-element.23.refs_2_, bf16[1,32,16,128]{3,2,1,0:T(8,128)(2,1)S(1)} %get-tuple-element.24.refs_3_, ...), custom_call_target="tpu_custom_call" | custom-call | tf_op jit(solution)/shard_map/pairs/pallas_call | solution.py:384
  (18 shorter events, 0.1 us)
Async XLA Ops:
  1.5 5.1 %collective-permute-start = (bf16[96,128]{1,0:T(8,128)(2,1)S(1)}, bf16[96,128]{1,0:T(8,128)(2,1)S(1)}, u32[]{:S(2)}, u32[]{:S(2)}) collective-permute-start(bf16[96,128]{1,0:T(8,128)(2,1)S(1)} %get-tuple-element.17), channel_id=1, source_target_pairs={{0,9},{1,8},{2,11},{3,10},{4,13},{5,12},{6,15},{7,14},{8,1},{9,0},... | collective-permute-start | bytes 73736 | tf_op jit(solution)/shard_map/ppermute | solution.py:344
  6.7 4.6 %collective-permute-start.1 = (bf16[96,128]{1,0:T(8,128)(2,1)S(1)}, bf16[96,128]{1,0:T(8,128)(2,1)S(1)}, u32[]{:S(2)}, u32[]{:S(2)}) collective-permute-start(bf16[96,128]{1,0:T(8,128)(2,1)S(1)} %get-tuple-element.18), channel_id=1, source_target_pairs={{0,5},{1,4},{2,1},{3,0},{4,7},{5,6},{6,3},{7,2},{8,13},{9,12},{10,... | collective-permute-start | bytes 73736 | tf_op jit(solution)/shard_map/ppermute | solution.py:344
  8.6 3.3 %collective-permute-start.2 = (bf16[96,128]{1,0:T(8,128)(2,1)S(1)}, bf16[96,128]{1,0:T(8,128)(2,1)S(1)}, u32[]{:S(2)}, u32[]{:S(2)}) collective-permute-start(bf16[96,128]{1,0:T(8,128)(2,1)S(1)} %get-tuple-element.19), channel_id=1, source_target_pairs={{0,3},{1,2},{2,7},{3,6},{4,1},{5,0},{6,5},{7,4},{8,11},{9,10},{10,... | collective-permute-start | bytes 73736 | tf_op jit(solution)/shard_map/ppermute | solution.py:344
  8.6 4.2 %collective-permute-start.3 = (bf16[96,128]{1,0:T(8,128)(2,1)S(1)}, bf16[96,128]{1,0:T(8,128)(2,1)S(1)}, u32[]{:S(2)}, u32[]{:S(2)}) collective-permute-start(bf16[96,128]{1,0:T(8,128)(2,1)S(1)} %get-tuple-element.20), channel_id=1, source_target_pairs={{0,7},{1,6},{2,5},{3,4},{4,3},{5,2},{6,1},{7,0},{8,15},{9,14},{10,... | collective-permute-start | bytes 73736 | tf_op jit(solution)/shard_map/ppermute | solution.py:344
  12.9 1.4 %collective-permute-start.4 = (bf16[256,128]{1,0:T(8,128)(2,1)S(1)}, bf16[256,128]{1,0:T(8,128)(2,1)S(1)}, u32[]{:S(2)}, u32[]{:S(2)}) collective-permute-start(bf16[256,128]{1,0:T(8,128)(2,1)S(1)} %constant_dynamic-update-slice_fusion.18), channel_id=1, source_target_pairs={{0,1},{1,0},{2,3},{3,2},{4,5},{5,4},{6,7},{7,6},{8,9},{9,8},{10,11... | collective-permute-start | bytes 196616 | tf_op jit(solution)/shard_map/ppermute | solution.py:344
